TPU v7x, 512 devices: a whole 4x8x8 slice. The times are simulated.
512 devices in a mesh: ctx: 32 (over x, z), inner: 16 (over y, core).
Axes of the slice: x: 4, y: 8, z: 8, core: 2. Of those that a mesh axis runs over, the one named last changes fastest.
Arguments:
- queries: bfloat16 [65536, 512], P(('ctx', 'inner')), may hold values from -8 to 8
- keys: bfloat16 [65536, 512], P(('ctx', 'inner')), may hold values from -6 to 6
- values: bfloat16 [65536, 512], P(('ctx', 'inner')), may hold values from -6 to 6
- w_proj: bfloat16 [8, 64, 256], replicated, may hold values from -1.5 to 1.5
- ln_gain: float32 [2, 64], replicated, may hold values from 0.1 to 1.9
- ln_bias: float32 [2, 64], replicated, may hold values from -3 to 3
- cotangent: bfloat16 [65536, 512], P(('ctx', 'inner')), may hold values from -6 to 6
Outputs:
- attended: bfloat16 [65536, 512], P(('ctx', 'inner'))
- grad_queries: bfloat16 [65536, 512], P(('ctx', 'inner'))
- grad_keys: bfloat16 [65536, 512], P(('ctx', 'inner'))
- grad_values: bfloat16 [65536, 512], P(('ctx', 'inner'))
- grad_proj: float32 [32, 8, 64, 256], P('ctx', None, None, 'inner')
- grad_norm: float32 [4, 64], replicated
All inputs are finite; a program needn't handle non-finite values.
Results may differ from a plain program's by a relative error of at most 0.012.
Values may be sent and summed in bfloat16 or wider, within the bound.
A program may use at most 64 MiB of HBM per device.

v0:
```python
import math

import jax
import jax.numpy as jnp
from jax import lax
from jax.sharding import Mesh
from jax.sharding import PartitionSpec as P

WIN = 128
CTX = ("ctx_0", "ctx_1")
INNER = ("inner_0", "inner_1")
CTX_INNER = ("ctx_0", "ctx_1", "inner_0", "inner_1")


def padded_2(x, sides, width):
    edges = {}
    for axis, dim in sides:
        size, length = (lax.axis_size(axis), x.shape[dim])
        up = [(i, (i + 1) % size) for i in range(size - 1)]
        last = lax.slice_in_dim(x, length - width, length, axis=dim)
        leading = lax.slice_in_dim(x, 0, width, axis=dim)
        edges[dim] = (
            lax.ppermute(last, axis, up),
            lax.ppermute(leading, axis, [(b, a) for a, b in up]),
        )
    done = []
    for _, dim in sides:
        low, high = edges[dim]
        around = [(width, width) if d in done else (0, 0) for d in range(x.ndim)]
        x = jnp.concatenate([jnp.pad(low, around), x, jnp.pad(high, around)], axis=dim)
        done.append(dim)
    return x


def copy_for_each(x, axis):
    copies = jnp.broadcast_to(x, (lax.axis_size(axis), *x.shape))
    return lax.all_to_all(copies, axis, split_axis=0, concat_axis=0, tiled=True)


def of_everyone(x, axis):
    return copy_for_each(x, axis).max(axis=0)


def over_axes(x, axes):
    far, near = axes
    return of_everyone(of_everyone(x, near), far)


def rows_for(lines, length):
    spare = -len(lines) % length
    return jnp.pad(lines, [(0, spare)] + [(0, 0)] * (lines.ndim - 1))


def in_order(blocks, dim):
    lengths = list(blocks.shape[1:])
    lengths[dim] *= blocks.shape[0]
    return jnp.moveaxis(blocks, 0, dim).reshape(lengths)


def gathered_by_axis(x, axes, dim):
    far, near = axes
    leading = copy_for_each(x, far)
    blocks = jnp.swapaxes(copy_for_each(leading, near), 0, 1)
    return in_order(blocks.reshape(-1, *x.shape), dim)


def split_up(x, dim, length):
    before, after = (x.shape[:dim], x.shape[dim + 1 :])
    return jnp.moveaxis(x.reshape(*before, length, -1, *after), dim, 0)


def summed_on_arrival(x, axis, dim):
    blocks = split_up(x, dim, lax.axis_size(axis))
    arrived = lax.all_to_all(blocks, axis, split_axis=0, concat_axis=0, tiled=True)
    return arrived.sum(axis=0)


def sum_in_two_steps(x, axes, dim):
    far, near = axes
    blocks = split_up(x, dim, lax.axis_size(far))
    nearer = summed_on_arrival(blocks, near, dim + 1)
    arrived = lax.all_to_all(nearer, far, split_axis=0, concat_axis=0, tiled=True)
    return arrived.sum(axis=0)


def total_of(x, axes):
    padded = rows_for(x, lax.axis_size(axes[0]) * lax.axis_size(axes[1]))
    whole = gathered_by_axis(sum_in_two_steps(padded, axes, 0), axes, 0)
    return lax.slice_in_dim(whole, 0, len(x)).reshape(x.shape)


def in_one(arrays, axis):
    ends = [0]
    for a in arrays:
        ends.append(ends[-1] + a.size)
    so_far = total_of(jnp.concatenate([a.ravel() for a in arrays]), axis)
    return tuple((so_far[b:e].reshape(a.shape) for a, b, e in zip(arrays, ends, ends[1:])))


def normalise(landmark, gain_row, bias_row):
    average = jnp.mean(landmark, axis=-1, keepdims=True)
    centred = landmark - average
    variance = jnp.mean(centred * centred, axis=-1, keepdims=True)
    inverse = 1.0 / jnp.sqrt(variance + 1e-05)
    normed = centred * inverse
    return (normed, inverse, normed * gain_row + bias_row)


def norm_backward(grad_out, normed, inverse, gain_row):
    grad_normed = grad_out * gain_row
    first_mean = jnp.mean(grad_normed, axis=-1, keepdims=True)
    second_mean = jnp.mean(grad_normed * normed, axis=-1, keepdims=True)
    grad_in = inverse * (grad_normed - first_mean - normed * second_mean)
    return (grad_in, jnp.sum(grad_out * normed, axis=(0, 1)), jnp.sum(grad_out, axis=(0, 1)))


def three_windows(padded, segments, window):
    span = segments * window
    leading = padded.shape[0]
    columns = padded.shape[-1]
    pieces = [
        padded[:, start : start + span].reshape(leading, segments, window, columns)
        for start in (0, window, 2 * window)
    ]
    return jnp.concatenate(pieces, axis=2)


def per_device(queries, keys, values, w_proj, ln_gain, ln_bias, cotangent):
    tokens_dev, features = queries.shape
    heads, head_dim, landmarks = w_proj.shape
    window = WIN
    segments = tokens_dev // window
    edge = 3 * window
    score_scale = 1.0 / math.sqrt(head_dim)
    devices = lax.axis_size(CTX) * lax.axis_size(INNER)
    position = lax.axis_index(CTX) * lax.axis_size(INNER) + lax.axis_index(INNER)
    kv_pad = padded_2(jnp.stack([keys, values]), ((CTX_INNER, 1),), window)
    kv_windows = three_windows(kv_pad, segments, window).reshape(2, segments, edge, heads, head_dim)
    key_window = kv_windows[0]
    value_window = kv_windows[1]
    neighbour = (
        position * segments
        + jnp.arange(segments)[:, None]
        - 1
        + jnp.arange(edge)[None, :] // window
    )
    usable = (neighbour >= 0) & (neighbour < devices * segments)
    key_heads = keys.reshape(tokens_dev, heads, head_dim)
    value_heads = values.reshape(tokens_dev, heads, head_dim)
    logits = jnp.einsum("thd,hdr->htr", key_heads, w_proj, preferred_element_type=jnp.float32)
    column_peak = over_axes(jnp.max(logits, axis=1), (("ctx_0", "ctx_1"), ("inner_0", "inner_1")))
    exponent = jnp.exp(logits - column_peak[:, None, :])
    narrowed = exponent.astype(jnp.bfloat16)
    key_sum = jnp.einsum("htr,thd->hrd", narrowed, key_heads, preferred_element_type=jnp.float32)
    value_sum = jnp.einsum(
        "htr,thd->hrd", narrowed, value_heads, preferred_element_type=jnp.float32
    )
    column_total, key_sum, value_sum = in_one(
        (jnp.sum(exponent, axis=1), key_sum, value_sum),
        (("ctx_0", "ctx_1"), ("inner_0", "inner_1")),
    )
    mean_keys = key_sum / column_total[..., None]
    mean_values = value_sum / column_total[..., None]
    normed_keys, inverse_keys, land_keys = normalise(mean_keys, ln_gain[0], ln_bias[0])
    normed_values, inverse_values, land_values = normalise(mean_values, ln_gain[1], ln_bias[1])
    land_key_b = land_keys.astype(jnp.bfloat16)
    land_value_b = land_values.astype(jnp.bfloat16)
    query_blocks = queries.reshape(segments, window, heads, head_dim)
    grad_blocks = cotangent.reshape(segments, window, heads, head_dim)
    window_scores = (
        jnp.einsum("sqhd,skhd->shqk", query_blocks, key_window, preferred_element_type=jnp.float32)
        * score_scale
    )
    window_scores = jnp.where(usable[:, None, None, :], window_scores, -1e30)
    land_scores = (
        jnp.einsum("sqhd,hrd->shqr", query_blocks, land_key_b, preferred_element_type=jnp.float32)
        * score_scale
    )
    scores = jnp.concatenate([window_scores, land_scores], axis=-1)
    row_peak = jnp.max(scores, axis=-1)
    log_total = row_peak + jnp.log(jnp.sum(jnp.exp(scores - row_peak[..., None]), axis=-1))
    probs = jnp.exp(scores - log_total[..., None])
    probs_b = probs.astype(jnp.bfloat16)
    output = jnp.einsum(
        "shqk,skhd->sqhd", probs_b[..., :edge], value_window, preferred_element_type=jnp.float32
    )
    output = output + jnp.einsum(
        "shqr,hrd->sqhd", probs_b[..., edge:], land_value_b, preferred_element_type=jnp.float32
    )
    attended = output.astype(jnp.bfloat16).reshape(tokens_dev, features)
    delta = jnp.sum(grad_blocks.astype(jnp.float32) * output, axis=-1).transpose(0, 2, 1)
    grad_window = jnp.einsum(
        "sqhd,skhd->shqk", grad_blocks, value_window, preferred_element_type=jnp.float32
    )
    grad_land = jnp.einsum(
        "sqhd,hrd->shqr", grad_blocks, land_value_b, preferred_element_type=jnp.float32
    )
    grad_probs = jnp.concatenate([grad_window, grad_land], axis=-1)
    grad_scores = (probs * (grad_probs - delta[..., None])).astype(jnp.bfloat16)
    grad_query = jnp.einsum(
        "shqk,skhd->sqhd", grad_scores[..., :edge], key_window, preferred_element_type=jnp.float32
    )
    grad_query = grad_query + jnp.einsum(
        "shqr,hrd->sqhd", grad_scores[..., edge:], land_key_b, preferred_element_type=jnp.float32
    )
    grad_queries = (grad_query * score_scale).astype(jnp.bfloat16).reshape(tokens_dev, features)
    land_key_grad = (
        jnp.einsum(
            "shqr,sqhd->hrd",
            grad_scores[..., edge:],
            query_blocks,
            preferred_element_type=jnp.float32,
        )
        * score_scale
    )
    land_value_grad = jnp.einsum(
        "shqr,sqhd->hrd", probs_b[..., edge:], grad_blocks, preferred_element_type=jnp.float32
    )
    land_key_grad, land_value_grad = in_one(
        (land_key_grad, land_value_grad), (("ctx_0", "ctx_1"), ("inner_0", "inner_1"))
    )
    query_pad = padded_2(jnp.stack([queries, cotangent]), ((CTX_INNER, 1),), window)
    query_windows = three_windows(query_pad, segments, window).reshape(
        2, segments, edge, heads, head_dim
    )
    stats = jnp.stack([log_total, delta]).transpose(0, 2, 1, 3).reshape(2, heads, tokens_dev)
    stat_pad = padded_2(stats, ((CTX_INNER, 2),), window)
    span = segments * window
    stat_pieces = [
        stat_pad[:, :, start : start + span].reshape(2, heads, segments, window)
        for start in (0, window, 2 * window)
    ]
    stat_windows = jnp.concatenate(stat_pieces, axis=3).transpose(0, 2, 1, 3)
    key_own = key_heads.reshape(segments, window, heads, head_dim)
    value_own = value_heads.reshape(segments, window, heads, head_dim)
    cross = (
        jnp.einsum("sjhd,sihd->shji", query_windows[0], key_own, preferred_element_type=jnp.float32)
        * score_scale
    )
    probs_cross = jnp.where(
        usable[:, None, :, None], jnp.exp(cross - stat_windows[0][..., None]), 0.0
    )
    grad_cross = jnp.einsum(
        "sjhd,sihd->shji", query_windows[1], value_own, preferred_element_type=jnp.float32
    )
    scores_cross = (probs_cross * (grad_cross - stat_windows[1][..., None])).astype(jnp.bfloat16)
    key_part = (
        jnp.einsum(
            "shji,sjhd->sihd", scores_cross, query_windows[0], preferred_element_type=jnp.float32
        )
        * score_scale
    )
    value_part = jnp.einsum(
        "shji,sjhd->sihd",
        probs_cross.astype(jnp.bfloat16),
        query_windows[1],
        preferred_element_type=jnp.float32,
    )
    window_grads = jnp.stack([key_part, value_part]).reshape(2, tokens_dev, features)
    grad_mean_keys, gain_key_grad, bias_key_grad = norm_backward(
        land_key_grad, normed_keys, inverse_keys, ln_gain[0]
    )
    grad_mean_values, gain_value_grad, bias_value_grad = norm_backward(
        land_value_grad, normed_values, inverse_values, ln_gain[1]
    )
    grad_norm = jnp.stack([gain_key_grad, bias_key_grad, gain_value_grad, bias_value_grad])
    grad_key_b = grad_mean_keys.astype(jnp.bfloat16)
    grad_value_b = grad_mean_values.astype(jnp.bfloat16)
    proj_grad = jnp.einsum(
        "thd,hrd->htr", key_heads, grad_key_b, preferred_element_type=jnp.float32
    )
    proj_grad = proj_grad + jnp.einsum(
        "thd,hrd->htr", value_heads, grad_value_b, preferred_element_type=jnp.float32
    )
    weights = narrowed.astype(jnp.float32) / column_total[:, None, :]
    column_sum = jnp.sum(grad_key_b.astype(jnp.float32) * mean_keys, axis=-1) + jnp.sum(
        grad_value_b.astype(jnp.float32) * mean_values, axis=-1
    )
    grad_logit = (weights * (proj_grad - column_sum[:, None, :])).astype(jnp.bfloat16)
    scaled_keys = (grad_mean_keys / column_total[..., None]).astype(jnp.bfloat16)
    scaled_values = (grad_mean_values / column_total[..., None]).astype(jnp.bfloat16)
    land_keys_grad = jnp.einsum(
        "htr,hrd->thd", narrowed, scaled_keys, preferred_element_type=jnp.float32
    )
    land_keys_grad = land_keys_grad + jnp.einsum(
        "htr,hdr->thd", grad_logit, w_proj, preferred_element_type=jnp.float32
    )
    land_values_grad = jnp.einsum(
        "htr,hrd->thd", narrowed, scaled_values, preferred_element_type=jnp.float32
    )
    grad_keys = (window_grads[0] + land_keys_grad.reshape(tokens_dev, features)).astype(
        jnp.bfloat16
    )
    grad_values = (window_grads[1] + land_values_grad.reshape(tokens_dev, features)).astype(
        jnp.bfloat16
    )
    weight_term = jnp.einsum(
        "thd,htr->hdr", key_heads, grad_logit, preferred_element_type=jnp.float32
    )
    grad_proj = summed_on_arrival(weight_term[None], INNER, 3)
    return (attended, grad_queries, grad_keys, grad_values, grad_proj, grad_norm)


def solution(mesh):
    finer = Mesh(mesh.devices.reshape(4, 8, 8, 2), ("ctx_0", "ctx_1", "inner_0", "inner_1"))
    in_specs = (
        P(CTX_INNER, None),
        P(CTX_INNER, None),
        P(CTX_INNER, None),
        P(),
        P(),
        P(),
        P(CTX_INNER, None),
    )
    out_specs = (
        P(CTX_INNER, None),
        P(CTX_INNER, None),
        P(CTX_INNER, None),
        P(CTX_INNER, None),
        P(CTX, None, None, INNER),
        P(),
    )
    return jax.shard_map(
        per_device, mesh=finer, in_specs=in_specs, out_specs=out_specs, check_vma=False
    )
```

profile of v0, /device:TPU:1, one launch (start us, length us, event | category | flops | bytes accessed | tf_op | source)
XLA Modules:
  0.0 353.8 jit_solution(1844222888345980871)
XLA Ops:
  2.1 18.5 %all_to_all.71 = f32[16,8,256]{2,1,0:T(8,128)S(1)} all-to-all(f32[16,8,256]{2,1,0:T(8,128)S(1)} %broadcast_in_dim.36), channel_id=1, replica_groups=mesh['ctx_0'=4,'ctx_1'=8,'inner_0'=8,'inner_1'=2] {'inner_0','inner_1'}, dimensions={0} | all-to-all | bytes 262144 | tf_op jit(solution)/shard_map/all_to_all | solution.py:37
  21.4 12.0 %all-to-all-start.1 = ((f32[32,8,256]{2,1,0:T(8,128)}), f32[32,8,256]{2,1,0:T(8,128)S(1)}, u32[]{:S(2)}, u32[]{:S(2)}) async-start(f32[32,8,256]{2,1,0:T(8,128)} %broadcast_in_dim.37), calls=%async_computation.1 | async-start | bytes 524288 | tf_op jit(solution)/shard_map/all_to_all | solution.py:37
  33.5 10.6 %all-to-all-done.1 = f32[32,8,256]{2,1,0:T(8,128)S(1)} async-done(((f32[32,8,256]{2,1,0:T(8,128)}), f32[32,8,256]{2,1,0:T(8,128)S(1)}, u32[]{:S(2)}, u32[]{:S(2)}) %all-to-all-start.1) | async-done | bytes 262176 | tf_op jit(solution)/shard_map/all_to_all | solution.py:37
  46.6 2.3 reshape_reshape.4
  49.3 38.9 %all_to_all.72 = f32[16,32,516]{2,1,0:T(8,128)S(1)} all-to-all(f32[16,32,516]{2,1,0:T(8,128)S(1)} %copy.172), channel_id=1, replica_groups=mesh['ctx_0'=4,'ctx_1'=8,'inner_0'=8,'inner_1'=2] {'inner_0','inner_1'}, dimensions={0} | all-to-all | bytes 2113536 | tf_op jit(solution)/shard_map/all_to_all | solution.py:74
  88.3 14.2 %all_to_all.73 = f32[32,1,516]{2,1,0:T(1,128)S(1)} all-to-all(f32[32,1,516]{2,1,0:T(1,128)S(1)} %all_to_all.48), channel_id=1, replica_groups=mesh['ctx_0'=4,'ctx_1'=8,'inner_0'=8,'inner_1'=2] {'ctx_0','ctx_1'}, dimensions={0} | all-to-all | bytes 132096 | tf_op jit(solution)/shard_map/all_to_all | solution.py:82
  102.6 12.5 %all_to_all.74 = f32[32,1,516]{2,1,0:T(1,128)S(1)} all-to-all(f32[32,1,516]{2,1,0:T(1,128)S(1)} %broadcast_in_dim.60), channel_id=1, replica_groups=mesh['ctx_0'=4,'ctx_1'=8,'inner_0'=8,'inner_1'=2] {'ctx_0','ctx_1'}, dimensions={0} | all-to-all | bytes 132096 | tf_op jit(solution)/shard_map/all_to_all | solution.py:37
  116.4 5.4 %all-to-all-start.5 = ((f32[16,32,516]{2,1,0:T(8,128)}), f32[16,32,516]{2,1,0:T(8,128)S(1)}, u32[]{:S(2)}, u32[]{:S(2)}) async-start(f32[16,32,516]{2,1,0:T(8,128)} %broadcast_in_dim.61), calls=%async_computation.5 | async-start | bytes 2621440 | tf_op jit(solution)/shard_map/all_to_all | solution.py:37
  121.8 2.1 collective-permute-start.1
  124.0 3.6 %collective-permute-start = (bf16[2,128,512]{2,1,0:T(8,128)(2,1)S(1)}, bf16[2,128,512]{2,1,0:T(8,128)(2,1)S(1)}, u32[]{:S(2)}, u32[]{:S(2)}) collective-permute-start(bf16[2,128,512]{2,1,0:T(8,128)(2,1)S(1)} %get-tuple-element.68), channel_id=1, source_target_pairs={{0,1},{1,2},{2,3},{3,4},{4,5},{5,6},{6,7},{7,8},{8,9},{9,10},{10,1... | collective-permute-start | bytes 786440 | tf_op jit(solution)/shard_map/ppermute | solution.py:23
  129.9 25.4 %collective-permute-done.1 = bf16[2,128,512]{2,1,0:T(8,128)(2,1)S(1)} collective-permute-done((bf16[2,128,512]{2,1,0:T(8,128)(2,1)S(1)}, bf16[2,128,512]{2,1,0:T(8,128)(2,1)S(1)}, u32[]{:S(2)}, u32[]{:S(2)}) %collective-permute-start.1) | collective-permute-done | bytes 262176 | tf_op jit(solution)/shard_map/ppermute | solution.py:24
  159.1 2.2 bitcast_reduce_fusion
  162.5 2.1 copy.173
  164.5 2.2 slice.86
  166.7 1.9 reshape_reshape.5
  176.6 2.0 convolution_bitcast_fusion.1
  178.6 2.2 convolution_bitcast_fusion.6
  182.1 2.4 concatenate.67
  184.4 2.5 multiply_reduce_fusion.10
  186.9 2.4 fusion.1
  196.8 6.4 %all-to-all-start.6 = ((f32[16,32,512]{2,1,0:T(8,128)}), f32[16,32,512]{2,1,0:T(8,128)S(1)}, u32[]{:S(2)}, u32[]{:S(2)}) async-start(f32[16,32,512]{2,1,0:T(8,128)} %copy.191), calls=%async_computation.6 | async-start | bytes 2097152 | tf_op jit(solution)/shard_map/all_to_all | solution.py:74
  203.2 1.9 fusion.32
  205.1 2.0 collective-permute-start.3
  207.1 3.6 %collective-permute-start.2 = (bf16[2,128,512]{2,1,0:T(8,128)(2,1)}, bf16[2,128,512]{2,1,0:T(8,128)(2,1)}, u32[]{:S(2)}, u32[]{:S(2)}) collective-permute-start(bf16[2,128,512]{2,1,0:T(8,128)(2,1)} %get-tuple-element.64), channel_id=1, source_target_pairs={{0,1},{1,2},{2,3},{3,4},{4,5},{5,6},{6,7},{7,8},{8,9},{9,10},{10,1... | collective-permute-start | bytes 786440 | tf_op jit(solution)/shard_map/ppermute | solution.py:23
  210.6 20.5 %all-to-all-done.6 = f32[16,32,512]{2,1,0:T(8,128)S(1)} async-done(((f32[16,32,512]{2,1,0:T(8,128)}), f32[16,32,512]{2,1,0:T(8,128)S(1)}, u32[]{:S(2)}, u32[]{:S(2)}) %all-to-all-start.6) | async-done | bytes 1048608 | tf_op jit(solution)/shard_map/all_to_all | solution.py:74
  233.4 4.3 %all-to-all-start.7 = ((f32[32,1,512]{2,1,0:T(1,128)}), f32[32,1,512]{2,1,0:T(1,128)S(1)}, u32[]{:S(2)}, u32[]{:S(2)}) async-start(f32[32,1,512]{2,1,0:T(1,128)} %all_to_all.54), calls=%async_computation.7 | async-start | bytes 131072 | tf_op jit(solution)/shard_map/all_to_all | solution.py:82
  238.8 8.2 %all-to-all-done.7 = f32[32,1,512]{2,1,0:T(1,128)S(1)} async-done(((f32[32,1,512]{2,1,0:T(1,128)}), f32[32,1,512]{2,1,0:T(1,128)S(1)}, u32[]{:S(2)}, u32[]{:S(2)}) %all-to-all-start.7) | async-done | bytes 65568 | tf_op jit(solution)/shard_map/all_to_all | solution.py:82
  247.8 3.9 %all-to-all-start.8 = ((f32[32,1,512]{2,1,0:T(1,128)}), f32[32,1,512]{2,1,0:T(1,128)S(1)}, u32[]{:S(2)}, u32[]{:S(2)}) async-start(f32[32,1,512]{2,1,0:T(1,128)} %broadcast_in_dim.63), calls=%async_computation.8 | async-start | bytes 131072 | tf_op jit(solution)/shard_map/all_to_all | solution.py:37
  252.6 2.0 copy.186
  254.5 2.0 copy.185
  256.5 3.5 slice.102
  260.6 2.3 collective-permute-start.5
  262.9 3.3 collective-permute-start.4
  267.3 4.2 %all-to-all-start.9 = ((f32[16,32,512]{2,1,0:T(8,128)}), f32[16,32,512]{2,1,0:T(8,128)S(1)}, u32[]{:S(2)}, u32[]{:S(2)}) async-start(f32[16,32,512]{2,1,0:T(8,128)} %broadcast_in_dim.64), calls=%async_computation.9 | async-start | bytes 2097152 | tf_op jit(solution)/shard_map/all_to_all | solution.py:37
  271.5 2.7 convolution_bitcast_fusion.5
  286.9 3.2 fusion.9
  291.9 7.5 %all-to-all-done.9 = f32[16,32,512]{2,1,0:T(8,128)S(1)} async-done(((f32[16,32,512]{2,1,0:T(8,128)}), f32[16,32,512]{2,1,0:T(8,128)S(1)}, u32[]{:S(2)}, u32[]{:S(2)}) %all-to-all-start.9) | async-done | bytes 1048608 | tf_op jit(solution)/shard_map/all_to_all | solution.py:37
  302.7 2.3 multiply_reduce_fusion.8
  307.3 2.3 reshape.574
  309.6 3.9 %fusion.21 = f32[8,64,128]{2,1,0:T(8,128)} fusion(bf16[8,128,256]{2,1,0:T(8,128)(2,1)} %copy-done.11, f32[8,256]{1,0:T(8,128)S(1)} %slice_bitcast_fusion.13, f32[8,256,64]{2,1,0:T(8,128)S(1)} %reshape.575, f32[8,256]{1,0:T(8,128)} %broadcast_multiply_fusion, f32[8,256]{1,0:T(8,128)} %broadcast_multiply_fusion.1, f32[64]{0:T(128)} %get-tuple-element.73, ...), kind=kOutput, calls=%fused_computation.70 | convolution fusion | flops 34865152 | bytes 1876224 | tf_op jit(solution)/shard_map/htr,hrd->thd/dot_general | solution.py:288
  313.6 3.7 %multiply_reduce_fusion.9 = (f32[8,256]{1,0:T(8,128)S(1)}, f32[8,256]{1,0:T(8,128)S(1)}, f32[64]{0:T(128)}, f32[8,256]{1,0:T(8,128)S(1)}, f32[64]{0:T(128)}) fusion(f32[8,256,64]{2,1,0:T(8,128)S(1)} %copy-done.4, f32[64]{0:T(128)S(1)} %copy-done.56, f32[8,256]{1,0:T(8,128)S(1)} %copy-done.38, f32[8,256]{1,0:T(8,128)S(1)} %get-tuple-element.85, ...), kind=kLoop, calls=%fused_computation.57 | loop fusion | flops 2877312 | bytes 2180096 | tf_op jit(solution)/shard_map/reduce_sum | solution.py:111
  317.3 2.6 multiply_reduce_fusion.1
  321.8 2.5 fusion.8
  326.7 2.8 reshape.579
  329.5 3.8 %all-to-all-start.10 = ((f32[16,1,8192]{2,1,0:T(1,128)}), f32[16,1,8192]{2,1,0:T(1,128)S(1)}, u32[]{:S(2)}, u32[]{:S(2)}) async-start(f32[16,1,8192]{2,1,0:T(1,128)} %reshape.579), calls=%async_computation.10 | async-start | bytes 1048576 | tf_op jit(solution)/shard_map/all_to_all | solution.py:74
  333.4 3.2 convolution_bitcast_fusion.4
  341.3 9.0 %all-to-all-done.10 = f32[16,1,8192]{2,1,0:T(1,128)S(1)} async-done(((f32[16,1,8192]{2,1,0:T(1,128)}), f32[16,1,8192]{2,1,0:T(1,128)S(1)}, u32[]{:S(2)}, u32[]{:S(2)}) %all-to-all-start.10) | async-done | bytes 524320 | tf_op jit(solution)/shard_map/all_to_all | solution.py:74
  350.8 1.9 reduce.10
  (239 shorter events, 67.8 us)
Async XLA Ops:
  0.6 32.7 %copy-start.31 = (bf16[128,512]{1,0:T(8,128)(2,1)S(1)}, bf16[128,512]{1,0:T(8,128)(2,1)}, u32[]{:S(2)}) copy-start(bf16[128,512]{1,0:T(8,128)(2,1)} %param.9) | copy-start | bytes 393220
  21.4 22.7 %all-to-all-start.1 = ((f32[32,8,256]{2,1,0:T(8,128)}), f32[32,8,256]{2,1,0:T(8,128)S(1)}, u32[]{:S(2)}, u32[]{:S(2)}) async-start(f32[32,8,256]{2,1,0:T(8,128)} %broadcast_in_dim.37), calls=%async_computation.1 | async-start | bytes 524288 | tf_op jit(solution)/shard_map/all_to_all | solution.py:37
  33.5 11.2 %copy-start.26 = (bf16[128,512]{0,1:T(8,128)(2,1)}, bf16[128,512]{0,1:T(8,128)(2,1)S(1)}, u32[]{:S(2)}) copy-start(bf16[128,512]{0,1:T(8,128)(2,1)S(1)} %copy.170) | copy-start | bytes 393220
  116.3 5.4 %copy-start.30 = (bf16[128,512]{1,0:T(8,128)(2,1)S(1)}, bf16[128,512]{1,0:T(8,128)(2,1)}, u32[]{:S(2)}) copy-start(bf16[128,512]{1,0:T(8,128)(2,1)} %param.8) | copy-start | bytes 393220
  116.3 5.4 %copy-start.32 = (bf16[128,512]{1,0:T(8,128)(2,1)S(1)}, bf16[128,512]{1,0:T(8,128)(2,1)}, u32[]{:S(2)}) copy-start(bf16[128,512]{1,0:T(8,128)(2,1)} %param.9) | copy-start | bytes 393220
  116.3 11.3 %copy-start.64 = (f32[2,64]{1,0:T(2,128)S(1)}, f32[2,64]{1,0:T(2,128)}, u32[]{:S(2)}) copy-start(f32[2,64]{1,0:T(2,128)} %param.11) | copy-start | bytes 1540
  116.3 11.9 %copy-start.23 = (bf16[128,512]{1,0:T(8,128)(2,1)S(1)}, bf16[128,512]{1,0:T(8,128)(2,1)}, u32[]{:S(2)}) copy-start(bf16[128,512]{1,0:T(8,128)(2,1)} %param.13) | copy-start | bytes 393220
  116.3 12.8 %copy-start.33 = (bf16[128,512]{1,0:T(8,128)(2,1)S(1)}, bf16[128,512]{1,0:T(8,128)(2,1)}, u32[]{:S(2)}) copy-start(bf16[128,512]{1,0:T(8,128)(2,1)} %param.7) | copy-start | bytes 393220
  116.3 12.9 %copy-start.65 = (f32[2,64]{1,0:T(2,128)S(1)}, f32[2,64]{1,0:T(2,128)}, u32[]{:S(2)}) copy-start(f32[2,64]{1,0:T(2,128)} %param.12) | copy-start | bytes 1540
  116.4 45.0 %all-to-all-start.5 = ((f32[16,32,516]{2,1,0:T(8,128)}), f32[16,32,516]{2,1,0:T(8,128)S(1)}, u32[]{:S(2)}, u32[]{:S(2)}) async-start(f32[16,32,516]{2,1,0:T(8,128)} %broadcast_in_dim.61), calls=%async_computation.5 | async-start | bytes 2621440 | tf_op jit(solution)/shard_map/all_to_all | solution.py:37
  121.8 33.5 %collective-permute-start.1 = (bf16[2,128,512]{2,1,0:T(8,128)(2,1)S(1)}, bf16[2,128,512]{2,1,0:T(8,128)(2,1)S(1)}, u32[]{:S(2)}, u32[]{:S(2)}) collective-permute-start(bf16[2,128,512]{2,1,0:T(8,128)(2,1)S(1)} %get-tuple-element.68), channel_id=1, source_target_pairs={{1,0},{2,1},{3,2},{4,3},{5,4},{6,5},{7,6},{8,7},{9,8},{10,9},{11,1... | collective-permute-start | bytes 786440 | tf_op jit(solution)/shard_map/ppermute | solution.py:24
  124.0 31.3 %collective-permute-start = (bf16[2,128,512]{2,1,0:T(8,128)(2,1)S(1)}, bf16[2,128,512]{2,1,0:T(8,128)(2,1)S(1)}, u32[]{:S(2)}, u32[]{:S(2)}) collective-permute-start(bf16[2,128,512]{2,1,0:T(8,128)(2,1)S(1)} %get-tuple-element.68), channel_id=1, source_target_pairs={{0,1},{1,2},{2,3},{3,4},{4,5},{5,6},{6,7},{7,8},{8,9},{9,10},{10,1... | collective-permute-start | bytes 786440 | tf_op jit(solution)/shard_map/ppermute | solution.py:23
  128.2 30.9 %copy-start.66 = (pred[384]{0:T(512)(128)(4,1)}, pred[384]{0:T(512)(128)(4,1)S(1)}, u32[]{:S(2)}) copy-start(pred[384]{0:T(512)(128)(4,1)S(1)} %compare_and_fusion) | copy-start | bytes 1156
  128.3 29.2 %copy-start.24 = (bf16[128,512]{0,1:T(8,128)(2,1)}, bf16[128,512]{0,1:T(8,128)(2,1)S(1)}, u32[]{:S(2)}) copy-start(bf16[128,512]{0,1:T(8,128)(2,1)S(1)} %copy.179) | copy-start | bytes 393220
  129.3 29.9 %copy-start.20 = (bf16[128,512]{0,1:T(8,128)(2,1)}, bf16[128,512]{0,1:T(8,128)(2,1)S(1)}, u32[]{:S(2)}) copy-start(bf16[128,512]{0,1:T(8,128)(2,1)S(1)} %copy.167) | copy-start | bytes 393220
  157.3 4.1 %copy-start.14 = (bf16[1,1,384,512]{2,3,1,0:T(8,128)(2,1)}, bf16[1,1,384,512]{2,3,1,0:T(8,128)(2,1)S(1)}, u32[]{:S(2)}) copy-start(bf16[1,1,384,512]{2,3,1,0:T(8,128)(2,1)S(1)} %copy.165) | copy-start | bytes 1179652
  164.5 4.1 %copy-start.3 = (f32[32,16,516]{2,1,0:T(8,128)}, f32[32,16,516]{2,1,0:T(8,128)S(1)}, u32[]{:S(2)}) copy-start(f32[32,16,516]{2,1,0:T(8,128)S(1)} %copy.173) | copy-start | bytes 3170308
  172.0 6.6 %copy-start.35 = (f32[8,256]{1,0:T(8,128)}, f32[8,256]{1,0:T(8,128)S(1)}, u32[]{:S(2)}) copy-start(f32[8,256]{1,0:T(8,128)S(1)} %get-tuple-element.84) | copy-start | bytes 24580
  173.8 4.8 %copy-start.40 = (f32[8,256]{1,0:T(8,128)}, f32[8,256]{1,0:T(8,128)S(1)}, u32[]{:S(2)}) copy-start(f32[8,256]{1,0:T(8,128)S(1)} %add_rsqrt_fusion) | copy-start | bytes 24580
  176.3 4.6 %copy-start.8 = (bf16[1,8,128,640]{2,3,1,0:T(8,128)(2,1)}, bf16[1,8,128,640]{2,3,1,0:T(8,128)(2,1)S(1)}, u32[]{:S(2)}) copy-start(bf16[1,8,128,640]{2,3,1,0:T(8,128)(2,1)S(1)} %fusion.2) | copy-start | bytes 3932164
  196.8 34.3 %all-to-all-start.6 = ((f32[16,32,512]{2,1,0:T(8,128)}), f32[16,32,512]{2,1,0:T(8,128)S(1)}, u32[]{:S(2)}, u32[]{:S(2)}) async-start(f32[16,32,512]{2,1,0:T(8,128)} %copy.191), calls=%async_computation.6 | async-start | bytes 2097152 | tf_op jit(solution)/shard_map/all_to_all | solution.py:74
  205.1 32.6 %collective-permute-start.3 = (bf16[2,128,512]{2,1,0:T(8,128)(2,1)}, bf16[2,128,512]{2,1,0:T(8,128)(2,1)}, u32[]{:S(2)}, u32[]{:S(2)}) collective-permute-start(bf16[2,128,512]{2,1,0:T(8,128)(2,1)} %get-tuple-element.64), channel_id=1, source_target_pairs={{1,0},{2,1},{3,2},{4,3},{5,4},{6,5},{7,6},{8,7},{9,8},{10,9},{11,1... | collective-permute-start | bytes 786440 | tf_op jit(solution)/shard_map/ppermute | solution.py:24
  207.1 30.6 %collective-permute-start.2 = (bf16[2,128,512]{2,1,0:T(8,128)(2,1)}, bf16[2,128,512]{2,1,0:T(8,128)(2,1)}, u32[]{:S(2)}, u32[]{:S(2)}) collective-permute-start(bf16[2,128,512]{2,1,0:T(8,128)(2,1)} %get-tuple-element.64), channel_id=1, source_target_pairs={{0,1},{1,2},{2,3},{3,4},{4,5},{5,6},{6,7},{7,8},{8,9},{9,10},{10,1... | collective-permute-start | bytes 786440 | tf_op jit(solution)/shard_map/ppermute | solution.py:23
  233.4 13.7 %all-to-all-start.7 = ((f32[32,1,512]{2,1,0:T(1,128)}), f32[32,1,512]{2,1,0:T(1,128)S(1)}, u32[]{:S(2)}, u32[]{:S(2)}) async-start(f32[32,1,512]{2,1,0:T(1,128)} %all_to_all.54), calls=%async_computation.7 | async-start | bytes 131072 | tf_op jit(solution)/shard_map/all_to_all | solution.py:82
  247.8 18.4 %all-to-all-start.8 = ((f32[32,1,512]{2,1,0:T(1,128)}), f32[32,1,512]{2,1,0:T(1,128)S(1)}, u32[]{:S(2)}, u32[]{:S(2)}) async-start(f32[32,1,512]{2,1,0:T(1,128)} %broadcast_in_dim.63), calls=%async_computation.8 | async-start | bytes 131072 | tf_op jit(solution)/shard_map/all_to_all | solution.py:37
  254.5 5.5 %copy-start.44 = (f32[8,128]{1,0:T(8,128)S(1)}, f32[8,128]{1,0:T(8,128)}, u32[]{:S(2)}) copy-start(f32[8,128]{1,0:T(8,128)} %copy-done.42) | copy-start | bytes 12292
  254.5 5.5 %copy-start.46 = (f32[128,8]{0,1:T(8,128)S(1)}, f32[128,8]{0,1:T(8,128)}, u32[]{:S(2)}) copy-start(f32[128,8]{0,1:T(8,128)} %copy-done.45) | copy-start | bytes 12292
  260.6 19.2 %collective-permute-start.5 = (f32[2,8,128]{2,1,0:T(8,128)}, f32[2,8,128]{2,1,0:T(8,128)}, u32[]{:S(2)}, u32[]{:S(2)}) collective-permute-start(f32[2,8,128]{2,1,0:T(8,128)} %get-tuple-element.72), channel_id=1, source_target_pairs={{1,0},{2,1},{3,2},{4,3},{5,4},{6,5},{7,6},{8,7},{9,8},{10,9},{11,1... | collective-permute-start | bytes 24584 | tf_op jit(solution)/shard_map/ppermute | solution.py:24
  262.9 16.9 %collective-permute-start.4 = (f32[2,8,128]{2,1,0:T(8,128)}, f32[2,8,128]{2,1,0:T(8,128)}, u32[]{:S(2)}, u32[]{:S(2)}) collective-permute-start(f32[2,8,128]{2,1,0:T(8,128)} %get-tuple-element.72), channel_id=1, source_target_pairs={{0,1},{1,2},{2,3},{3,4},{4,5},{5,6},{6,7},{7,8},{8,9},{9,10},{10,1... | collective-permute-start | bytes 24584 | tf_op jit(solution)/shard_map/ppermute | solution.py:23
  267.3 32.1 %all-to-all-start.9 = ((f32[16,32,512]{2,1,0:T(8,128)}), f32[16,32,512]{2,1,0:T(8,128)S(1)}, u32[]{:S(2)}, u32[]{:S(2)}) async-start(f32[16,32,512]{2,1,0:T(8,128)} %broadcast_in_dim.64), calls=%async_computation.9 | async-start | bytes 2097152 | tf_op jit(solution)/shard_map/all_to_all | solution.py:37
  279.8 4.4 %copy-start.17 = (bf16[1,1,384,512]{2,3,1,0:T(8,128)(2,1)S(1)}, bf16[1,1,384,512]{2,3,1,0:T(8,128)(2,1)}, u32[]{:S(2)}) copy-start(bf16[1,1,384,512]{2,3,1,0:T(8,128)(2,1)} %copy.186) | copy-start | bytes 1179652
  309.6 4.0 %copy-start.36 = (f32[8,256]{1,0:T(8,128)S(1)}, f32[8,256]{1,0:T(8,128)}, u32[]{:S(2)}) copy-start(f32[8,256]{1,0:T(8,128)} %copy-done.35) | copy-start | bytes 24580
  309.6 4.0 %copy-start.38 = (f32[8,256]{1,0:T(8,128)S(1)}, f32[8,256]{1,0:T(8,128)}, u32[]{:S(2)}) copy-start(f32[8,256]{1,0:T(8,128)} %copy-done.37) | copy-start | bytes 24580
  309.6 4.0 %copy-start.41 = (f32[8,256]{1,0:T(8,128)S(1)}, f32[8,256]{1,0:T(8,128)}, u32[]{:S(2)}) copy-start(f32[8,256]{1,0:T(8,128)} %copy-done.40) | copy-start | bytes 24580
  309.6 4.0 %copy-start.51 = (f32[8,256]{1,0:T(8,128)S(1)}, f32[8,256]{1,0:T(8,128)}, u32[]{:S(2)}) copy-start(f32[8,256]{1,0:T(8,128)} %broadcast_multiply_fusion.1) | copy-start | bytes 24580
  309.6 4.0 %copy-start.52 = (f32[8,256]{1,0:T(8,128)S(1)}, f32[8,256]{1,0:T(8,128)}, u32[]{:S(2)}) copy-start(f32[8,256]{1,0:T(8,128)} %broadcast_multiply_fusion) | copy-start | bytes 24580
  309.6 4.0 %copy-start.56 = (f32[64]{0:T(128)S(1)}, f32[64]{0:T(128)}, u32[]{:S(2)}) copy-start(f32[64]{0:T(128)} %get-tuple-element.74) | copy-start | bytes 772
  309.6 4.0 %copy-start.59 = (f32[64]{0:T(128)S(1)}, f32[64]{0:T(128)}, u32[]{:S(2)}) copy-start(f32[64]{0:T(128)} %get-tuple-element.73) | copy-start | bytes 772
  317.3 4.4 %copy-start.47 = (f32[8,256]{1,0:T(8,128)}, f32[8,256]{1,0:T(8,128)S(1)}, u32[]{:S(2)}) copy-start(f32[8,256]{1,0:T(8,128)S(1)} %broadcast_multiply_fusion.3) | copy-start | bytes 24580
  317.3 4.4 %copy-start.49 = (f32[8,256]{1,0:T(8,128)}, f32[8,256]{1,0:T(8,128)S(1)}, u32[]{:S(2)}) copy-start(f32[8,256]{1,0:T(8,128)S(1)} %broadcast_multiply_fusion.2) | copy-start | bytes 24580
  326.7 6.6 %copy-start.5 = (f32[8,256,64]{2,1,0:T(8,128)S(1)}, f32[8,256,64]{2,1,0:T(8,128)}, u32[]{:S(2)}) copy-start(f32[8,256,64]{2,1,0:T(8,128)} %reshape.574) | copy-start | bytes 1572868
  326.7 6.6 %copy-start.13 = (bf16[8,128,256]{2,1,0:T(8,128)(2,1)S(1)}, bf16[8,128,256]{2,1,0:T(8,128)(2,1)}, u32[]{:S(2)}) copy-start(bf16[8,128,256]{2,1,0:T(8,128)(2,1)} %copy-done.11) | copy-start | bytes 1572868
  326.7 6.6 %copy-start.39 = (f32[8,256]{1,0:T(8,128)S(1)}, f32[8,256]{1,0:T(8,128)}, u32[]{:S(2)}) copy-start(f32[8,256]{1,0:T(8,128)} %copy-done.37) | copy-start | bytes 24580
  326.7 6.6 %copy-start.48 = (f32[8,256]{1,0:T(8,128)S(1)}, f32[8,256]{1,0:T(8,128)}, u32[]{:S(2)}) copy-start(f32[8,256]{1,0:T(8,128)} %copy-done.47) | copy-start | bytes 24580
  326.7 6.6 %copy-start.50 = (f32[8,256]{1,0:T(8,128)S(1)}, f32[8,256]{1,0:T(8,128)}, u32[]{:S(2)}) copy-start(f32[8,256]{1,0:T(8,128)} %copy-done.49) | copy-start | bytes 24580
  326.7 6.6 %copy-start.57 = (f32[64]{0:T(128)S(1)}, f32[64]{0:T(128)}, u32[]{:S(2)}) copy-start(f32[64]{0:T(128)} %get-tuple-element.74) | copy-start | bytes 772
  329.5 20.8 %all-to-all-start.10 = ((f32[16,1,8192]{2,1,0:T(1,128)}), f32[16,1,8192]{2,1,0:T(1,128)S(1)}, u32[]{:S(2)}, u32[]{:S(2)}) async-start(f32[16,1,8192]{2,1,0:T(1,128)} %reshape.579), calls=%async_computation.10 | async-start | bytes 1048576 | tf_op jit(solution)/shard_map/all_to_all | solution.py:74
  336.6 4.0 %copy-start.29 = (f32[128,512]{1,0:T(8,128)S(1)}, f32[128,512]{1,0:T(8,128)}, u32[]{:S(2)}) copy-start(f32[128,512]{1,0:T(8,128)} %copy.200) | copy-start | bytes 786436
  (34 other events, 66.6 us)
where the time goes:
time: 356 us; the launch traced here: 354 us
  blocking collectives  84 us (24%)
  waiting for transfers between devices  81.2 us (23%)
  local copies, waits for them, and re-layouts  63.5 us (18%)
  starting transfers between devices  56.7 us (16%)
  matrix products  37.5 us (11%)
  other arithmetic  29.2 us (8%)
    all_to_all x1, blocking collectives, summed_on_arrival(): lax.all_to_all(blocks, axis, split_axis=0, concat_axis=0, tiled=True)  38.9 us
    all_to_all x2, blocking collectives, copy_for_each(): return lax.all_to_all(copies, axis, split_axis=0, concat_axis=0, tiled=True)  31 us
    all_to_all x2, waiting for transfers between devices, summed_on_arrival(): lax.all_to_all(blocks, axis, split_axis=0, concat_axis=0, tiled=True)  29.5 us
    ppermute x3, waiting for transfers between devices, padded_2(): lax.ppermute(leading, axis, [(b, a) for a, b in up])  25.4 us
    all_to_all x4, starting transfers between devices, copy_for_each(): return lax.all_to_all(copies, axis, split_axis=0, concat_axis=0, tiled=True)  25.4 us
    all_to_all x4, waiting for transfers between devices, copy_for_each(): return lax.all_to_all(copies, axis, split_axis=0, concat_axis=0, tiled=True)  18.1 us
    all_to_all x1, blocking collectives, sum_in_two_steps(): lax.all_to_all(nearer, far, split_axis=0, concat_axis=0, tiled=True)  14.2 us
    unnamed x149, local copies, waits for them, and re-layouts  14.1 us
  transfers between devices with their start and end apart: 13, of which 6 were waited for; matrix products, arithmetic and copies ran while one was open for 14% of the time, Pallas kernels for 0%

commit v1 on v0

v1 whole, which is shorter than its diff:
```python
import functools
import types

import jax
import jax.numpy as jnp
from jax import lax
from jax.experimental import pallas as pl
from jax.experimental.pallas import tpu as pltpu
from jax.sharding import Mesh
from jax.sharding import PartitionSpec as P

AXES = ("x", "z", "y", "c")
WIN = 128
DH = 64
LANDMARKS = 256
F32 = jnp.float32
BF16 = jnp.bfloat16


def rcopy(src, dst, send, recv, device):
    return pltpu.make_async_remote_copy(
        src_ref=src,
        dst_ref=dst,
        send_sem=send,
        recv_sem=recv,
        device_id=device,
        device_id_type=pl.DeviceIdType.MESH,
    )


def mm(a, b):
    return lax.dot_general(a, b, (((1,), (0,)), ((), ())), preferred_element_type=F32)


def mm_t(a, b):
    return lax.dot_general(a, b, (((1,), (1,)), ((), ())), preferred_element_type=F32)


def left_half(shape):
    return lax.broadcasted_iota(jnp.int32, shape, 1) < DH


def half_mean(x):
    left = left_half(x.shape)
    low = jnp.sum(jnp.where(left, x, 0.0), axis=1, keepdims=True)
    high = jnp.sum(jnp.where(left, 0.0, x), axis=1, keepdims=True)
    return jnp.where(left, low, high) * (1.0 / DH)


def pack_heads(a_ref, b_ref, pair):
    cols = pl.ds(pair * WIN, WIN)
    a, b = a_ref[:, cols].astype(F32), b_ref[:, cols].astype(F32)
    left = left_half(a.shape)
    even = jnp.where(left, a, pltpu.roll(b, DH, 1)).astype(BF16)
    odd = jnp.where(left, pltpu.roll(a, DH, 1), b).astype(BF16)
    return even, odd


def unpack_heads(even, odd):
    even, odd = even.astype(F32), odd.astype(F32)
    left = left_half(even.shape)
    a = jnp.where(left, even, pltpu.roll(odd, DH, 1)).astype(BF16)
    b = jnp.where(left, pltpu.roll(even, DH, 1), odd).astype(BF16)
    return a, b


def as_row(col, base):
    shape = (col.shape[0], WIN)
    diag = lax.broadcasted_iota(jnp.int32, shape, 1) == lax.broadcasted_iota(jnp.int32, shape, 0) + base
    return jnp.sum(jnp.where(diag, col, 0.0), axis=0, keepdims=True)


def as_col(row, n, base):
    shape = (n, WIN)
    diag = lax.broadcasted_iota(jnp.int32, shape, 1) == lax.broadcasted_iota(jnp.int32, shape, 0) + base
    return jnp.sum(jnp.where(diag, row, 0.0), axis=1, keepdims=True)


def combine(parts):
    peak = functools.reduce(jnp.maximum, [log_weight for _, log_weight in parts])
    scaled = [(mean, jnp.exp(log_weight - peak)) for mean, log_weight in parts]
    total = functools.reduce(lambda a, b: a + b, [w for _, w in scaled])
    mean = functools.reduce(lambda a, b: a + b, [m * w for m, w in scaled])
    return mean / total, peak + jnp.log(total)


def kernel(dims, names, *refs):
    X, Z, Y, C = dims
    R = types.SimpleNamespace(**dict(zip(names, refs)))
    NS = Y
    G = 2 * X
    CH = LANDMARKS // G
    N = 2 * Y
    POS = X * Z * 2
    x, z, y, c = (lax.axis_index(a) for a in AXES)
    r = x * 2 + c
    n = y * 2 + c
    g = x * Z + z
    pos = g * 2 + c

    def inner_dev(m):
        return (x, z, m // 2, lax.rem(m, 2))

    def plane_dev(o):
        p = lax.rem(r + o, G)
        return (p // 2, z, y, lax.rem(p, 2))

    def z_dev(o):
        return (x, lax.rem(z + o, Z), y, c)

    def chain_dev(q):
        q = lax.rem(q + POS, POS)
        return (q // (2 * Z), lax.rem(q // 2, Z), y, lax.rem(q, 2))

    far = chain_dev(pos + 2 * c - 1)
    right_dev, left_dev = chain_dev(pos + 1), chain_dev(pos - 1)

    barrier = pltpu.get_barrier_semaphore()
    count = 0
    for o in range(1, N):
        pl.semaphore_signal(barrier, 1, device_id=inner_dev(lax.rem(n + o, N)), device_id_type=pl.DeviceIdType.MESH)
        count += 1
    for xo in range(1, X):
        for c2 in range(2):
            pl.semaphore_signal(
                barrier, 1, device_id=(lax.rem(x + xo, X), z, y, c2), device_id_type=pl.DeviceIdType.MESH
            )
            count += 1
    for o in range(1, Z):
        pl.semaphore_signal(barrier, 1, device_id=z_dev(o), device_id_type=pl.DeviceIdType.MESH)
        count += 1
    pl.semaphore_signal(barrier, 1, device_id=far, device_id_type=pl.DeviceIdType.MESH)
    count += 1

    for pair in range(Y // 2):
        R.kvm[2 * pair], R.kvm[2 * pair + 1] = pack_heads(R.k, R.v, pair)
    pl.semaphore_wait(barrier, count)

    half = Y // 2
    core_in = y // half
    slot_in = lax.rem(y, half) * 2 + c
    self_in = c == core_in

    def send_in(src, dst, base, send, recv):
        for o in range(Y):
            to = lax.rem(y + o, Y)
            remote = rcopy(src.at[to], dst.at[base + slot_in], send.at[o], recv.at[slot_in], (x, z, to, core_in))
            if o:
                remote.start()
            else:
                pl.when(jnp.logical_not(self_in))(remote.start)

                @pl.when(self_in)
                def _():
                    pltpu.make_async_copy(src.at[y], dst.at[base + slot_in], recv.at[slot_in]).start()

    def sent_in(src, dst, base, send, recv):
        for o in range(Y):
            to = lax.rem(y + o, Y)
            remote = rcopy(src.at[to], dst.at[base + slot_in], send.at[o], recv.at[slot_in], (x, z, to, core_in))
            if o:
                remote.wait_send()
            else:
                pl.when(jnp.logical_not(self_in))(remote.wait_send)

    def received(src, dst, base, send, recv, j):
        rcopy(src.at[0], dst.at[base + j], send.at[0], recv.at[j], (x, z, y, c)).wait_recv()

    kv_move = (R.kvm, R.kvx, 1, R.kv_s, R.kv_r)
    qg_move = (R.qgm, R.qg, 0, R.qg_s, R.qg_r)
    send_in(*kv_move)
    for pair in range(Y // 2):
        R.qgm[2 * pair], R.qgm[2 * pair + 1] = pack_heads(R.q, R.g, pair)
    send_in(*qg_move)

    w_pad = jnp.concatenate([R.w[y], jnp.zeros((DH, LANDMARKS), BF16)], axis=0)
    R.wp[...] = w_pad
    R.wt[...] = w_pad.astype(F32).T.astype(BF16)
    gain = jnp.concatenate([R.gain[0:1, :], R.gain[1:2, :]], axis=1)
    bias = jnp.concatenate([R.bias[0:1, :], R.bias[1:2, :]], axis=1)

    for j in range(NS):
        received(*kv_move, j)

    kv_own = R.kvx[1 : NS + 1].reshape(NS * WIN, WIN)
    logits = mm_t(R.wt[...], kv_own)
    peak = jnp.max(logits, axis=1, keepdims=True)
    expo = jnp.exp(logits - peak)
    total = jnp.sum(expo, axis=1, keepdims=True)
    means = mm(expo.astype(BF16), kv_own) / total
    log_weights = peak + jnp.log(total)
    for p in range(G):
        rows = slice(p * CH, (p + 1) * CH)
        R.s1[p, 0:CH] = means[rows]
        R.s1[p, CH : CH + 8] = jnp.broadcast_to(as_row(log_weights[rows], 0), (8, WIN))

    def plane(send, o):
        return lax.rem(r + o, G)

    def scatter_copies(src, dst, send, recv):
        return [
            rcopy(src.at[lax.rem(r + o, G)], dst.at[o - 1], send.at[o - 1], recv.at[o - 1], plane_dev(o))
            for o in range(1, G)
        ]

    def z_copies(src, dst, send, recv):
        return [rcopy(src, dst.at[o - 1], send.at[o - 1], recv.at[o - 1], z_dev(o)) for o in range(1, Z)]

    def gather_copies(buf, send, recv):
        return [
            rcopy(buf.at[r], buf.at[r], send.at[o - 1], recv.at[o - 1], plane_dev(o)) for o in range(1, G)
        ]

    pending = []

    def start(copies):
        for copy in copies:
            copy.start()
        pending.extend(copies)
        return copies

    def arrive(copies):
        for copy in copies:
            copy.wait_recv()

    scatter_1 = start(scatter_copies(R.s1, R.r1, R.s1_s, R.s1_r))

    halo = start(
        [
            rcopy(R.kvx.at[NS], R.kvx.at[0], R.h_s.at[0], R.h_r.at[0], right_dev),
            rcopy(R.kvx.at[1], R.kvx.at[NS + 1], R.h_s.at[1], R.h_r.at[1], left_dev),
        ]
    )

    def transpose_kv(s):
        R.kvt[:, s * WIN : (s + 1) * WIN] = R.kvx[s].astype(F32).T.astype(BF16)

    for s in range(1, NS + 1):
        transpose_kv(s)

    def part_of(ref, o):
        return (ref[o, 0:CH], as_col(ref[o, CH : CH + 1], CH, 0))

    arrive(scatter_1)
    mean, log_weight = combine([part_of(R.s1, r)] + [part_of(R.r1, o) for o in range(G - 1)])
    R.s2[0:CH] = mean
    R.s2[CH : CH + 8] = jnp.broadcast_to(as_row(log_weight, 0), (8, WIN))
    z_1 = start(z_copies(R.s2, R.r2, R.s2_s, R.s2_r))

    arrive(halo)
    transpose_kv(0)
    transpose_kv(NS + 1)

    def window_scores(s):
        received(*qg_move, s)
        qg = R.qg[s]
        left = left_half(qg.shape)
        zero = jnp.zeros_like(qg)
        R.rr[s, 0:WIN] = jnp.where(left, qg * jnp.asarray(0.125, BF16), zero)
        R.rr[s, WIN : 2 * WIN] = jnp.where(left, zero, qg)
        R.gt[s] = qg.astype(F32).T[DH:]
        kv = R.kvx[s : s + 3].reshape(3 * WIN, WIN)
        both = mm_t(kv, R.rr[s])
        scores = both[:, 0:WIN]
        if s == 0:
            rows = lax.broadcasted_iota(jnp.int32, (3 * WIN, 1), 0)
            scores = scores + jnp.where((rows < WIN) & (pos == 0), -1e30, 0.0)
        if s == NS - 1:
            rows = lax.broadcasted_iota(jnp.int32, (3 * WIN, 1), 0)
            scores = scores + jnp.where((rows >= 2 * WIN) & (pos == POS - 1), -1e30, 0.0)
        R.sw[s] = scores
        R.gpw[s] = both[:, WIN:]
        top = jnp.max(scores, axis=0, keepdims=True)
        weight = jnp.exp(scores - top)
        R.mw[s] = jnp.broadcast_to(top, (8, WIN))
        R.lw[s] = jnp.broadcast_to(jnp.sum(weight, axis=0, keepdims=True), (8, WIN))
        R.ow[s] = mm(R.kvt[:, s * WIN : (s + 3) * WIN], weight.astype(BF16))

    split = (NS + 1) // 2
    for s in range(split):
        window_scores(s)

    arrive(z_1)
    mean, log_weight = combine(
        [(mean, log_weight)] + [part_of(R.r2, o) for o in range(Z - 1)]
    )
    centred = mean - half_mean(mean)
    inverse = 1.0 / jnp.sqrt(half_mean(centred * centred) + 1e-05)
    normed = centred * inverse
    R.land[r] = (normed * gain + bias).astype(BF16)
    gather_1 = start(gather_copies(R.land, R.g1_s, R.g1_r))
    base = lax.rem(r * CH, WIN)
    R.lt[r] = jnp.broadcast_to(as_row(log_weight, base), (8, WIN))
    gather_l = start(gather_copies(R.lt, R.gl_s, R.gl_r))

    for s in range(split, NS):
        window_scores(s)

    arrive(gather_1)

    land = R.land[...].reshape(LANDMARKS, WIN)
    land_t = land.astype(F32).T.astype(BF16)
    R.landt[...] = land_t
    for s in range(NS):
        both = mm_t(land, R.rr[s])
        scores = both[:, 0:WIN]
        top_w = R.mw[s, 0:1]
        top = jnp.maximum(top_w, jnp.max(scores, axis=0, keepdims=True))
        weight = jnp.exp(scores - top)
        shrink = jnp.exp(top_w - top)
        total = R.lw[s, 0:1] * shrink + jnp.sum(weight, axis=0, keepdims=True)
        per = 1.0 / total
        probs = weight * per
        probs_b = probs.astype(BF16)
        out_t = R.ow[s] * (shrink * per) + mm(land_t, probs_b)
        delta = jnp.sum(out_t[DH:] * R.gt[s], axis=0, keepdims=True)
        grad = (probs * (both[:, WIN:] - delta)).astype(BF16)
        R.dp[:, 2 * s * WIN : (2 * s + 1) * WIN] = grad
        R.dp[:, (2 * s + 1) * WIN : (2 * s + 2) * WIN] = probs_b
        R.ow[s] = out_t
        R.mw[s] = jnp.broadcast_to(top + jnp.log(total), (8, WIN))
        R.lw[s] = jnp.broadcast_to(delta, (8, WIN))
    R.s3[...] = mm(R.dp[...], R.rr[...].reshape(2 * NS * WIN, WIN)).reshape(G, CH, WIN)
    scatter_2 = start(scatter_copies(R.s3, R.r3, R.s3_s, R.s3_r))

    R.dkv[...] = jnp.zeros_like(R.dkv)

    def out_copy(s):
        seg = c * NS + s
        return rcopy(R.om.at[s], R.oi.at[y], R.o_s.at[s], R.o_r.at[y], (x, z, seg // 2, lax.rem(seg, 2)))

    def is_own(s):
        return n == c * NS + s

    def send_out(s, src, dst, send, recv):
        seg = c * NS + s
        copy = rcopy(src.at[s], dst.at[y], send.at[s], recv.at[y], (x, z, seg // 2, lax.rem(seg, 2)))
        pl.when(jnp.logical_not(is_own(s)))(copy.start)

        @pl.when(is_own(s))
        def _():
            pltpu.make_async_copy(src.at[s], dst.at[y], recv.at[y]).start()

    def sent_out(s, src, dst, send, recv):
        seg = c * NS + s
        copy = rcopy(src.at[s], dst.at[y], send.at[s], recv.at[y], (x, z, seg // 2, lax.rem(seg, 2)))
        pl.when(jnp.logical_not(is_own(s)))(copy.wait_send)

    def window_grads(s):
        probs = jnp.exp(R.sw[s] - R.mw[s, 0:1])
        grad = (probs * (R.gpw[s] - R.lw[s, 0:1])).astype(BF16)
        both = jnp.concatenate([grad, probs.astype(BF16)], axis=1)
        part = mm(both, R.rr[s])
        for i in range(3):
            R.dkv[s + i] += part[i * WIN : (i + 1) * WIN]
        grad_q = mm(R.kvt[:, s * WIN : (s + 3) * WIN], grad) + mm(
            R.landt[...], R.dp[:, 2 * s * WIN : (2 * s + 1) * WIN]
        )
        rows = lax.broadcasted_iota(jnp.int32, (WIN, WIN), 0) < DH
        packed = jnp.where(rows, grad_q * 0.125, R.ow[s])
        R.om[s] = packed.T.astype(BF16)
        send_out(s, R.om, R.oi, R.o_s, R.o_r)

    for s in range(split):
        window_grads(s)
    arrive(scatter_2)
    land_grad = R.s3[r]
    for o in range(G - 1):
        land_grad = land_grad + R.r3[o]
    R.s4[...] = land_grad
    z_2 = start(z_copies(R.s4, R.r4, R.s4_s, R.s4_r))
    for s in range(split, NS):
        window_grads(s)
    back = start(
        [
            rcopy(R.dkv.at[NS + 1], R.dh.at[0], R.d_s.at[0], R.d_r.at[0], right_dev),
            rcopy(R.dkv.at[0], R.dh.at[1], R.d_s.at[1], R.d_r.at[1], left_dev),
        ]
    )
    arrive(z_2)
    for o in range(Z - 1):
        land_grad = land_grad + R.r4[o]
    scaled = land_grad * gain
    grad_mean = inverse * (scaled - half_mean(scaled) - normed * half_mean(scaled * normed))
    grad_mean_b = grad_mean.astype(BF16)
    R.gkv[r] = grad_mean_b
    gather_2 = start(gather_copies(R.gkv, R.g2_s, R.g2_r))
    column = jnp.sum(grad_mean_b.astype(F32) * mean, axis=1, keepdims=True)
    R.ct[r] = jnp.concatenate(
        [
            as_row(column, base),
            jnp.sum(land_grad * normed, axis=0, keepdims=True),
            jnp.sum(land_grad, axis=0, keepdims=True),
            jnp.zeros((5, WIN), F32),
        ],
        axis=0,
    )
    gather_c = start(gather_copies(R.ct, R.gc_s, R.gc_r))

    def row_of(ref):
        per = WIN // CH
        rows = []
        for first in range(0, G, per):
            rows.append(functools.reduce(lambda a, b: a + b, [ref[p, 0:1] for p in range(first, first + per)]))
        return jnp.concatenate(rows, axis=1)

    arrive(gather_l)
    log_row = row_of(R.lt)
    for s in range(NS):
        R.wgt[s] = jnp.exp(mm(R.kvx[s + 1], R.wp[...]) - log_row)
    arrive(back)
    R.dkv[1] += R.dh[0]
    R.dkv[NS] += R.dh[1]

    for h in range(Y):
        rcopy(R.om.at[0], R.oi.at[h], R.o_s.at[0], R.o_r.at[h], (x, z, y, c)).wait_recv()
    for pair in range(Y // 2):
        cols = slice(pair * WIN, (pair + 1) * WIN)
        R.gq_o[:, cols], R.att_o[:, cols] = unpack_heads(R.oi[2 * pair], R.oi[2 * pair + 1])

    arrive(gather_2)
    arrive(gather_c)
    column_row = row_of(R.ct)
    grads = R.gkv[...].reshape(LANDMARKS, WIN)
    stacked = jnp.concatenate([grads, R.wt[...]], axis=0)
    for s in range(NS):
        weight = R.wgt[s]
        grad = (weight * (mm_t(R.kvx[s + 1], grads) - column_row)).astype(BF16)
        R.dl[s] = grad
        both = jnp.concatenate([weight.astype(BF16), grad], axis=1)
        R.km[s] = (mm(both, stacked) + R.dkv[s + 1]).astype(BF16)
        send_out(s, R.km, R.ki, R.k_s, R.k_r)
    proj = mm(R.kvt[:, WIN : (NS + 1) * WIN], R.dl[...].reshape(NS * WIN, LANDMARKS)).T
    LN = LANDMARKS // N
    norm_tile = functools.reduce(lambda a, b: a + b, [R.ct[p] for p in range(G)])
    for m in range(N):
        R.pm[m, 0:LN] = proj[m * LN : (m + 1) * LN]
        R.pm[m, LN : LN + 8] = norm_tile
    proj_copies = start(
        [
            rcopy(R.pm.at[lax.rem(n + o, N)], R.pi.at[n], R.p_s.at[o - 1], R.p_r.at[o - 1], inner_dev(lax.rem(n + o, N)))
            for o in range(1, N)
        ]
    )
    R.pi[n] = R.pm[n]
    for h in range(Y):
        rcopy(R.km.at[0], R.ki.at[h], R.k_s.at[0], R.k_r.at[h], (x, z, y, c)).wait_recv()
    for pair in range(Y // 2):
        cols = slice(pair * WIN, (pair + 1) * WIN)
        R.gk_o[:, cols], R.gv_o[:, cols] = unpack_heads(R.ki[2 * pair], R.ki[2 * pair + 1])
    arrive(proj_copies)
    for h in range(Y):
        R.gp_o[h] = R.pi[2 * h, 0:LN] + R.pi[2 * h + 1, 0:LN]
    sums = functools.reduce(lambda a, b: a + b, [R.pi[2 * h, LN : LN + 8] for h in range(Y)])
    R.gn_o[0:1] = sums[1:2, 0:DH]
    R.gn_o[1:2] = sums[2:3, 0:DH]
    R.gn_o[2:3] = sums[1:2, DH:]
    R.gn_o[3:4] = sums[2:3, DH:]

    sent_in(*kv_move)
    sent_in(*qg_move)
    for s in range(NS):
        sent_out(s, R.om, R.oi, R.o_s, R.o_r)
        sent_out(s, R.km, R.ki, R.k_s, R.k_r)
    for copy in pending:
        copy.wait_send()


def layer(dims, q, k, v, w, gain, bias, g):
    X, Z, Y, C = dims
    NS, G, N = Y, 2 * X, 2 * Y
    CH, LN = LANDMARKS // G, LANDMARKS // N
    block = (WIN, WIN)
    dma = pltpu.SemaphoreType.DMA
    scratch = dict(
        kvm=((Y, *block), BF16),
        qgm=((Y, *block), BF16),
        kvx=((NS + 2, *block), BF16),
        qg=((NS, *block), BF16),
        wp=((WIN, LANDMARKS), BF16),
        wt=((LANDMARKS, WIN), BF16),
        s1=((G, CH + 8, WIN), F32),
        r1=((G - 1, CH + 8, WIN), F32),
        s2=((CH + 8, WIN), F32),
        r2=((Z - 1, CH + 8, WIN), F32),
        kvt=((WIN, (NS + 2) * WIN), BF16),
        rr=((NS, 2 * WIN, WIN), BF16),
        gt=((NS, DH, WIN), F32),
        sw=((NS, 3 * WIN, WIN), F32),
        gpw=((NS, 3 * WIN, WIN), F32),
        mw=((NS, 8, WIN), F32),
        lw=((NS, 8, WIN), F32),
        ow=((NS, *block), F32),
        land=((G, CH, WIN), BF16),
        lt=((G, 8, WIN), F32),
        landt=((WIN, LANDMARKS), BF16),
        dp=((LANDMARKS, 2 * NS * WIN), BF16),
        s3=((G, CH, WIN), F32),
        r3=((G - 1, CH, WIN), F32),
        s4=((CH, WIN), F32),
        r4=((Z - 1, CH, WIN), F32),
        dkv=((NS + 2, *block), F32),
        dh=((2, *block), F32),
        om=((NS, *block), BF16),
        oi=((Y, *block), BF16),
        gkv=((G, CH, WIN), BF16),
        ct=((G, 8, WIN), F32),
        wgt=((NS, WIN, LANDMARKS), F32),
        dl=((NS, WIN, LANDMARKS), BF16),
        km=((NS, *block), BF16),
        ki=((Y, *block), BF16),
        pm=((N, LN + 8, WIN), F32),
        pi=((N, LN + 8, WIN), F32),
    )
    counts = dict(
        kv=Y, qg=Y, h=2, s1=G - 1, s2=Z - 1, g1=G - 1, gl=G - 1, s3=G - 1, s4=Z - 1, g2=G - 1, gc=G - 1,
        d=2, o=Y, k=Y, p=N - 1,
    )
    sems = {f"{name}_{side}": dma((count,)) for name, count in counts.items() for side in "sr"}
    outs = dict(
        att_o=((WIN, Y * DH), BF16),
        gq_o=((WIN, Y * DH), BF16),
        gk_o=((WIN, Y * DH), BF16),
        gv_o=((WIN, Y * DH), BF16),
        gp_o=((Y, LN, WIN), F32),
        gn_o=((4, DH), F32),
    )
    names = ("q", "k", "v", "w", "gain", "bias", "g", *outs, *scratch, *sems)
    att, gq, gk, gv, gp, gn = pl.pallas_call(
        functools.partial(kernel, dims, names),
        out_shape=[jax.ShapeDtypeStruct(*o) for o in outs.values()],
        in_specs=[pl.BlockSpec(memory_space=pltpu.VMEM)] * 7,
        out_specs=[pl.BlockSpec(memory_space=pltpu.VMEM)] * len(outs),
        scratch_shapes=[pltpu.VMEM(*s) for s in scratch.values()] + list(sems.values()),
        compiler_params=pltpu.CompilerParams(
            collective_id=0, has_side_effects=True, vmem_limit_bytes=40 * 1024 * 1024
        ),
    )(q, k, v, w, gain, bias, g)
    return att, gq, gk, gv, gp[:, :, :DH].transpose(0, 2, 1)[None], gn


def build(devices):
    finer = Mesh(devices, AXES)
    tokens = P(AXES, None)
    return jax.shard_map(
        functools.partial(layer, devices.shape),
        mesh=finer,
        in_specs=(tokens, tokens, tokens, P(), P(), P(), tokens),
        out_specs=(tokens, tokens, tokens, tokens, P(("x", "z"), None, None, ("y", "c")), P()),
        check_vma=False,
    )


def solution(mesh):
    return build(mesh.devices.reshape(4, 8, 8, 2))
```

time: 356 us -> 83.3 us (0.23)
  blocking collectives: 84 us -> 0 us
  waiting for transfers between devices: 81.2 us -> 0 us
  Pallas kernels: 0 us -> 72.7 us
  starting transfers between devices: 56.7 us -> 0 us
  local copies, waits for them, and re-layouts: 63.5 us -> 9.75 us
  matrix products: 37.5 us -> 0 us
  other arithmetic: 29.2 us -> 0 us
    all_to_all x4 -> x0, blocking collectives: 84 us -> none  [the longest x1 38.9 us: summed_on_arrival(): lax.all_to_all(blocks, axis, split_axis=0, concat_axis=0, tiled=True)]
    pallas_call x0 -> x1, Pallas kernels: none -> 72.7 us  [layer(): pl.pallas_call(functools.partial(kernel, dims, names), out_shape=[jax.Sha...]
    all_to_all x7 -> x0, waiting for transfers between devices: 55.8 us -> none  [the longest x2 29.5 us: summed_on_arrival(): lax.all_to_all(blocks, axis, split_axis=0, concat_axis=0, tiled=True)]
    all_to_all x7 -> x0, starting transfers between devices: 39.8 us -> none  [the longest x4 25.4 us: copy_for_each(): return lax.all_to_all(copies, axis, split_axis=0, concat_axis=0, tiled=True)]
    dot_general x22 -> x0, matrix products: 37.5 us -> none  [the longest x1 3.9 us: per_device(): jnp.einsum('htr,hrd->thd', narrowed, scaled_values, preferred_element_typ...]
    ppermute x6 -> x0, waiting for transfers between devices: 25.4 us -> none  [the longest x3 25.4 us: padded_2(): lax.ppermute(leading, axis, [(b, a) for a, b in up])]
    ppermute x6 -> x0, starting transfers between devices: 16.8 us -> none  [the longest x3 10.4 us: padded_2(): lax.ppermute(last, axis, up)]
    slice x12 -> x0, local copies, waits for them, and re-layouts: 15.3 us -> none  [the longest x6 10 us: in_one(): so_far[b:e].reshape(a.shape)]
  transfers between devices with their start and end apart: 13 -> 0, of which waited for: 6 -> 0; matrix products, arithmetic and copies ran while one was open for 14% -> 0% of each run, Pallas kernels for 0% -> 0%
where the time goes in v1:
time: 83.3 us; the launch traced here: 83.1 us
  Pallas kernels  72.7 us (87%)
  local copies, waits for them, and re-layouts  9.75 us (12%)
    pallas_call x1, Pallas kernels, layer(): pl.pallas_call(functools.partial(kernel, dims, names), out_shape=[jax.Sha...  72.7 us
    unnamed x19, local copies, waits for them, and re-layouts  9.11 us

profile of v1, /device:TPU:1, one launch (start us, length us, event | category | flops | bytes accessed | tf_op | source)
XLA Modules:
  0.0 83.1 jit_solution(13673410572267792302)
XLA Ops:
  0.6 0.0 copy-start
  0.6 0.9 %copy-done = bf16[8,64,256]{2,1,0:T(8,128)(2,1)S(1)} copy-done((bf16[8,64,256]{2,1,0:T(8,128)(2,1)S(1)}, bf16[8,64,256]{2,1,0:T(8,128)(2,1)}, u32[]{:S(2)}) %copy-start) | copy-done | bytes 262168
  1.6 0.0 copy-start.1
  1.6 0.9 %copy-done.1 = bf16[128,512]{1,0:T(8,128)(2,1)S(1)} copy-done((bf16[128,512]{1,0:T(8,128)(2,1)S(1)}, bf16[128,512]{1,0:T(8,128)(2,1)}, u32[]{:S(2)}) %copy-start.1) | copy-done | bytes 131096
  2.5 0.0 copy-start.2
  2.5 0.9 %copy-done.2 = bf16[128,512]{1,0:T(8,128)(2,1)S(1)} copy-done((bf16[128,512]{1,0:T(8,128)(2,1)S(1)}, bf16[128,512]{1,0:T(8,128)(2,1)}, u32[]{:S(2)}) %copy-start.2) | copy-done | bytes 131096
  3.4 0.0 copy-start.3
  3.4 0.9 %copy-done.3 = bf16[128,512]{1,0:T(8,128)(2,1)S(1)} copy-done((bf16[128,512]{1,0:T(8,128)(2,1)S(1)}, bf16[128,512]{1,0:T(8,128)(2,1)}, u32[]{:S(2)}) %copy-start.3) | copy-done | bytes 131096
  4.3 0.0 copy-start.4
  4.3 0.9 %copy-done.4 = bf16[128,512]{1,0:T(8,128)(2,1)S(1)} copy-done((bf16[128,512]{1,0:T(8,128)(2,1)S(1)}, bf16[128,512]{1,0:T(8,128)(2,1)}, u32[]{:S(2)}) %copy-start.4) | copy-done | bytes 131096
  5.2 0.0 copy-start.5
  5.2 0.7 copy-done.5
  5.9 0.0 copy-start.6
  5.9 0.7 copy-done.6
  6.6 72.7 %shard_map.118 = (bf16[128,512]{1,0:T(8,128)(2,1)S(1)}, bf16[128,512]{1,0:T(8,128)(2,1)S(1)}, bf16[128,512]{1,0:T(8,128)(2,1)S(1)}, bf16[128,512]{1,0:T(8,128)(2...) custom-call(bf16[128,512]{1,0:T(8,128)(2,1)S(1)} %copy-done.1, bf16[128,512]{1,0:T(8,128)(2,1)S(1)} %copy-done.2, ...), custom_call_target="tpu_custom_call" | custom-call | tf_op jit(solution)/shard_map/pallas_call | solution.py:529
  79.3 0.6 slice_bitcast_fusion
  79.9 0.7 copy.18
  80.6 0.7 copy.19
  81.2 0.7 copy.20
  81.9 0.7 copy.21
  82.5 0.6 copy.22
Async XLA Ops:
  0.6 1.0 %copy-start = (bf16[8,64,256]{2,1,0:T(8,128)(2,1)S(1)}, bf16[8,64,256]{2,1,0:T(8,128)(2,1)}, u32[]{:S(2)}) copy-start(bf16[8,64,256]{2,1,0:T(8,128)(2,1)} %refs_3_.1) | copy-start | bytes 786436
  1.6 0.9 %copy-start.1 = (bf16[128,512]{1,0:T(8,128)(2,1)S(1)}, bf16[128,512]{1,0:T(8,128)(2,1)}, u32[]{:S(2)}) copy-start(bf16[128,512]{1,0:T(8,128)(2,1)} %refs_0_.1) | copy-start | bytes 393220
  2.5 0.9 %copy-start.2 = (bf16[128,512]{1,0:T(8,128)(2,1)S(1)}, bf16[128,512]{1,0:T(8,128)(2,1)}, u32[]{:S(2)}) copy-start(bf16[128,512]{1,0:T(8,128)(2,1)} %refs_1_.1) | copy-start | bytes 393220
  3.4 0.9 %copy-start.3 = (bf16[128,512]{1,0:T(8,128)(2,1)S(1)}, bf16[128,512]{1,0:T(8,128)(2,1)}, u32[]{:S(2)}) copy-start(bf16[128,512]{1,0:T(8,128)(2,1)} %refs_2_.1) | copy-start | bytes 393220
  4.3 0.9 %copy-start.4 = (bf16[128,512]{1,0:T(8,128)(2,1)S(1)}, bf16[128,512]{1,0:T(8,128)(2,1)}, u32[]{:S(2)}) copy-start(bf16[128,512]{1,0:T(8,128)(2,1)} %refs_6_.1) | copy-start | bytes 393220
  5.2 0.7 copy-start.5
  5.9 0.7 copy-start.6

commit v2 on v1

--- a/solution.py
+++ b/solution.py
@@ -114,6 +114,22 @@
 
     far = chain_dev(pos + 2 * c - 1)
     right_dev, left_dev = chain_dev(pos + 1), chain_dev(pos - 1)
+
+    stores = {}
+
+    def store(*which):
+        for name in which:
+            stores[name] = pltpu.make_async_copy(
+                getattr(R, name + "_b"), getattr(R, name + "_o"), R.out_s.at[len(stores)]
+            )
+            stores[name].start()
+
+    loads = {}
+    for i, (name, src) in enumerate(
+        (("k", R.k_i), ("v", R.v_i), ("q", R.q_i), ("g", R.g_i), ("w", R.w_i.at[y]), ("gain", R.gain_i), ("bias", R.bias_i))
+    ):
+        loads[name] = pltpu.make_async_copy(src, getattr(R, name), R.in_s.at[i])
+        loads[name].start()
 
     barrier = pltpu.get_barrier_semaphore()
     count = 0
@@ -132,10 +148,13 @@
     pl.semaphore_signal(barrier, 1, device_id=far, device_id_type=pl.DeviceIdType.MESH)
     count += 1
 
+    loads["k"].wait()
+    loads["v"].wait()
     for pair in range(Y // 2):
         R.kvm[2 * pair], R.kvm[2 * pair + 1] = pack_heads(R.k, R.v, pair)
     pl.semaphore_wait(barrier, count)
 
+    unsent = []
     half = Y // 2
     core_in = y // half
     slot_in = lax.rem(y, half) * 2 + c
@@ -147,33 +166,30 @@
             remote = rcopy(src.at[to], dst.at[base + slot_in], send.at[o], recv.at[slot_in], (x, z, to, core_in))
             if o:
                 remote.start()
+                unsent.append(remote.wait_send)
             else:
                 pl.when(jnp.logical_not(self_in))(remote.start)
+                unsent.append(functools.partial(pl.when(jnp.logical_not(self_in)), remote.wait_send))
 
                 @pl.when(self_in)
                 def _():
                     pltpu.make_async_copy(src.at[y], dst.at[base + slot_in], recv.at[slot_in]).start()
 
-    def sent_in(src, dst, base, send, recv):
-        for o in range(Y):
-            to = lax.rem(y + o, Y)
-            remote = rcopy(src.at[to], dst.at[base + slot_in], send.at[o], recv.at[slot_in], (x, z, to, core_in))
-            if o:
-                remote.wait_send()
-            else:
-                pl.when(jnp.logical_not(self_in))(remote.wait_send)
-
     def received(src, dst, base, send, recv, j):
         rcopy(src.at[0], dst.at[base + j], send.at[0], recv.at[j], (x, z, y, c)).wait_recv()
 
     kv_move = (R.kvm, R.kvx, 1, R.kv_s, R.kv_r)
     qg_move = (R.qgm, R.qg, 0, R.qg_s, R.qg_r)
     send_in(*kv_move)
+    loads["q"].wait()
+    loads["g"].wait()
     for pair in range(Y // 2):
         R.qgm[2 * pair], R.qgm[2 * pair + 1] = pack_heads(R.q, R.g, pair)
     send_in(*qg_move)
 
-    w_pad = jnp.concatenate([R.w[y], jnp.zeros((DH, LANDMARKS), BF16)], axis=0)
+    for name in ("w", "gain", "bias"):
+        loads[name].wait()
+    w_pad = jnp.concatenate([R.w[...], jnp.zeros((DH, LANDMARKS), BF16)], axis=0)
     R.wp[...] = w_pad
     R.wt[...] = w_pad.astype(F32).T.astype(BF16)
     gain = jnp.concatenate([R.gain[0:1, :], R.gain[1:2, :]], axis=1)
@@ -194,9 +210,6 @@
         R.s1[p, 0:CH] = means[rows]
         R.s1[p, CH : CH + 8] = jnp.broadcast_to(as_row(log_weights[rows], 0), (8, WIN))
 
-    def plane(send, o):
-        return lax.rem(r + o, G)
-
     def scatter_copies(src, dst, send, recv):
         return [
             rcopy(src.at[lax.rem(r + o, G)], dst.at[o - 1], send.at[o - 1], recv.at[o - 1], plane_dev(o))
@@ -211,12 +224,10 @@
             rcopy(buf.at[r], buf.at[r], send.at[o - 1], recv.at[o - 1], plane_dev(o)) for o in range(1, G)
         ]
 
-    pending = []
-
     def start(copies):
         for copy in copies:
             copy.start()
-        pending.extend(copies)
+            unsent.append(copy.wait_send)
         return copies
 
     def arrive(copies):
@@ -251,34 +262,40 @@
     transpose_kv(0)
     transpose_kv(NS + 1)
 
-    def window_scores(s):
-        received(*qg_move, s)
-        qg = R.qg[s]
-        left = left_half(qg.shape)
-        zero = jnp.zeros_like(qg)
-        R.rr[s, 0:WIN] = jnp.where(left, qg * jnp.asarray(0.125, BF16), zero)
-        R.rr[s, WIN : 2 * WIN] = jnp.where(left, zero, qg)
-        R.gt[s] = qg.astype(F32).T[DH:]
-        kv = R.kvx[s : s + 3].reshape(3 * WIN, WIN)
-        both = mm_t(kv, R.rr[s])
-        scores = both[:, 0:WIN]
-        if s == 0:
-            rows = lax.broadcasted_iota(jnp.int32, (3 * WIN, 1), 0)
-            scores = scores + jnp.where((rows < WIN) & (pos == 0), -1e30, 0.0)
-        if s == NS - 1:
-            rows = lax.broadcasted_iota(jnp.int32, (3 * WIN, 1), 0)
-            scores = scores + jnp.where((rows >= 2 * WIN) & (pos == POS - 1), -1e30, 0.0)
-        R.sw[s] = scores
-        R.gpw[s] = both[:, WIN:]
-        top = jnp.max(scores, axis=0, keepdims=True)
-        weight = jnp.exp(scores - top)
-        R.mw[s] = jnp.broadcast_to(top, (8, WIN))
-        R.lw[s] = jnp.broadcast_to(jnp.sum(weight, axis=0, keepdims=True), (8, WIN))
-        R.ow[s] = mm(R.kvt[:, s * WIN : (s + 3) * WIN], weight.astype(BF16))
+    def window_scores(segs):
+        for s in segs:
+            received(*qg_move, s)
+        for s in segs:
+            qg = R.qg[s]
+            left = left_half(qg.shape)
+            zero = jnp.zeros_like(qg)
+            R.rr[s, 0:WIN] = jnp.where(left, qg * jnp.asarray(0.125, BF16), zero)
+            R.rr[s, WIN : 2 * WIN] = jnp.where(left, zero, qg)
+        for s in segs:
+            R.gt[s] = R.qg[s].astype(F32).T[DH:]
+        for s in segs:
+            both = mm_t(R.kvx[s : s + 3].reshape(3 * WIN, WIN), R.rr[s])
+            scores = both[:, 0:WIN]
+            if s == 0:
+                rows = lax.broadcasted_iota(jnp.int32, (3 * WIN, 1), 0)
+                scores = scores + jnp.where((rows < WIN) & (pos == 0), -1e30, 0.0)
+            if s == NS - 1:
+                rows = lax.broadcasted_iota(jnp.int32, (3 * WIN, 1), 0)
+                scores = scores + jnp.where((rows >= 2 * WIN) & (pos == POS - 1), -1e30, 0.0)
+            R.sw[s] = scores
+            R.gpw[s] = both[:, WIN:]
+        tops = {s: jnp.max(R.sw[s], axis=0, keepdims=True) for s in segs}
+        weights = {}
+        for s in segs:
+            weight = jnp.exp(R.sw[s] - tops[s])
+            R.mw[s] = jnp.broadcast_to(tops[s], (8, WIN))
+            R.lw[s] = jnp.broadcast_to(jnp.sum(weight, axis=0, keepdims=True), (8, WIN))
+            weights[s] = weight.astype(BF16)
+        for s in segs:
+            R.ow[s] = mm(R.kvt[:, s * WIN : (s + 3) * WIN], weights[s])
 
     split = (NS + 1) // 2
-    for s in range(split):
-        window_scores(s)
+    window_scores(range(split))
 
     arrive(z_1)
     mean, log_weight = combine(
@@ -293,41 +310,34 @@
     R.lt[r] = jnp.broadcast_to(as_row(log_weight, base), (8, WIN))
     gather_l = start(gather_copies(R.lt, R.gl_s, R.gl_r))
 
-    for s in range(split, NS):
-        window_scores(s)
+    window_scores(range(split, NS))
 
     arrive(gather_1)
 
     land = R.land[...].reshape(LANDMARKS, WIN)
     land_t = land.astype(F32).T.astype(BF16)
     R.landt[...] = land_t
-    for s in range(NS):
-        both = mm_t(land, R.rr[s])
-        scores = both[:, 0:WIN]
-        top_w = R.mw[s, 0:1]
-        top = jnp.maximum(top_w, jnp.max(scores, axis=0, keepdims=True))
-        weight = jnp.exp(scores - top)
-        shrink = jnp.exp(top_w - top)
-        total = R.lw[s, 0:1] * shrink + jnp.sum(weight, axis=0, keepdims=True)
-        per = 1.0 / total
-        probs = weight * per
-        probs_b = probs.astype(BF16)
-        out_t = R.ow[s] * (shrink * per) + mm(land_t, probs_b)
-        delta = jnp.sum(out_t[DH:] * R.gt[s], axis=0, keepdims=True)
-        grad = (probs * (both[:, WIN:] - delta)).astype(BF16)
-        R.dp[:, 2 * s * WIN : (2 * s + 1) * WIN] = grad
-        R.dp[:, (2 * s + 1) * WIN : (2 * s + 2) * WIN] = probs_b
-        R.ow[s] = out_t
-        R.mw[s] = jnp.broadcast_to(top + jnp.log(total), (8, WIN))
-        R.lw[s] = jnp.broadcast_to(delta, (8, WIN))
+    every = range(NS)
+    both = [mm_t(land, R.rr[s]) for s in every]
+    tops = [jnp.maximum(R.mw[s, 0:1], jnp.max(both[s][:, 0:WIN], axis=0, keepdims=True)) for s in every]
+    weights = [jnp.exp(both[s][:, 0:WIN] - tops[s]) for s in every]
+    shrinks = [jnp.exp(R.mw[s, 0:1] - tops[s]) for s in every]
+    totals = [R.lw[s, 0:1] * shrinks[s] + jnp.sum(weights[s], axis=0, keepdims=True) for s in every]
+    pers = [1.0 / t for t in totals]
+    probs = [w * per for w, per in zip(weights, pers)]
+    for s in every:
+        R.dp[:, (2 * s + 1) * WIN : (2 * s + 2) * WIN] = probs[s].astype(BF16)
+        R.mw[s] = jnp.broadcast_to(tops[s] + jnp.log(totals[s]), (8, WIN))
+    for s in every:
+        R.ow[s] = R.ow[s] * (shrinks[s] * pers[s]) + mm(land_t, R.dp[:, (2 * s + 1) * WIN : (2 * s + 2) * WIN])
+    deltas = [jnp.sum(R.ow[s, DH:] * R.gt[s], axis=0, keepdims=True) for s in every]
+    for s in every:
+        R.dp[:, 2 * s * WIN : (2 * s + 1) * WIN] = (probs[s] * (both[s][:, WIN:] - deltas[s])).astype(BF16)
+        R.lw[s] = jnp.broadcast_to(deltas[s], (8, WIN))
     R.s3[...] = mm(R.dp[...], R.rr[...].reshape(2 * NS * WIN, WIN)).reshape(G, CH, WIN)
     scatter_2 = start(scatter_copies(R.s3, R.r3, R.s3_s, R.s3_r))
 
     R.dkv[...] = jnp.zeros_like(R.dkv)
-
-    def out_copy(s):
-        seg = c * NS + s
-        return rcopy(R.om.at[s], R.oi.at[y], R.o_s.at[s], R.o_r.at[y], (x, z, seg // 2, lax.rem(seg, 2)))
 
     def is_own(s):
         return n == c * NS + s
@@ -336,41 +346,42 @@
         seg = c * NS + s
         copy = rcopy(src.at[s], dst.at[y], send.at[s], recv.at[y], (x, z, seg // 2, lax.rem(seg, 2)))
         pl.when(jnp.logical_not(is_own(s)))(copy.start)
+        unsent.append(functools.partial(pl.when(jnp.logical_not(is_own(s))), copy.wait_send))
 
         @pl.when(is_own(s))
         def _():
             pltpu.make_async_copy(src.at[s], dst.at[y], recv.at[y]).start()
 
-    def sent_out(s, src, dst, send, recv):
-        seg = c * NS + s
-        copy = rcopy(src.at[s], dst.at[y], send.at[s], recv.at[y], (x, z, seg // 2, lax.rem(seg, 2)))
-        pl.when(jnp.logical_not(is_own(s)))(copy.wait_send)
-
-    def window_grads(s):
-        probs = jnp.exp(R.sw[s] - R.mw[s, 0:1])
-        grad = (probs * (R.gpw[s] - R.lw[s, 0:1])).astype(BF16)
-        both = jnp.concatenate([grad, probs.astype(BF16)], axis=1)
-        part = mm(both, R.rr[s])
-        for i in range(3):
-            R.dkv[s + i] += part[i * WIN : (i + 1) * WIN]
-        grad_q = mm(R.kvt[:, s * WIN : (s + 3) * WIN], grad) + mm(
-            R.landt[...], R.dp[:, 2 * s * WIN : (2 * s + 1) * WIN]
-        )
+    def window_grads(segs):
+        grads, probs_b = {}, {}
+        for s in segs:
+            probs = jnp.exp(R.sw[s] - R.mw[s, 0:1])
+            grads[s] = (probs * (R.gpw[s] - R.lw[s, 0:1])).astype(BF16)
+            probs_b[s] = probs.astype(BF16)
+        for s in segs:
+            part = mm(jnp.concatenate([grads[s], probs_b[s]], axis=1), R.rr[s])
+            for i in range(3):
+                R.dkv[s + i] += part[i * WIN : (i + 1) * WIN]
         rows = lax.broadcasted_iota(jnp.int32, (WIN, WIN), 0) < DH
-        packed = jnp.where(rows, grad_q * 0.125, R.ow[s])
-        R.om[s] = packed.T.astype(BF16)
-        send_out(s, R.om, R.oi, R.o_s, R.o_r)
-
-    for s in range(split):
-        window_grads(s)
+        packed = []
+        for s in segs:
+            grad_q = mm(R.kvt[:, s * WIN : (s + 3) * WIN], grads[s]) + mm(
+                R.landt[...], R.dp[:, 2 * s * WIN : (2 * s + 1) * WIN]
+            )
+            packed.append(jnp.where(rows, grad_q * 0.125, R.ow[s]))
+        for s, block in zip(segs, packed):
+            R.om[s] = block.T.astype(BF16)
+        for s in segs:
+            send_out(s, R.om, R.oi, R.o_s, R.o_r)
+
+    window_grads(range(split))
     arrive(scatter_2)
     land_grad = R.s3[r]
     for o in range(G - 1):
         land_grad = land_grad + R.r3[o]
     R.s4[...] = land_grad
     z_2 = start(z_copies(R.s4, R.r4, R.s4_s, R.s4_r))
-    for s in range(split, NS):
-        window_grads(s)
+    window_grads(range(split, NS))
     back = start(
         [
             rcopy(R.dkv.at[NS + 1], R.dh.at[0], R.d_s.at[0], R.d_r.at[0], right_dev),
@@ -416,20 +427,23 @@
         rcopy(R.om.at[0], R.oi.at[h], R.o_s.at[0], R.o_r.at[h], (x, z, y, c)).wait_recv()
     for pair in range(Y // 2):
         cols = slice(pair * WIN, (pair + 1) * WIN)
-        R.gq_o[:, cols], R.att_o[:, cols] = unpack_heads(R.oi[2 * pair], R.oi[2 * pair + 1])
+        R.gq_b[:, cols], R.att_b[:, cols] = unpack_heads(R.oi[2 * pair], R.oi[2 * pair + 1])
+    store("gq", "att")
 
     arrive(gather_2)
     arrive(gather_c)
     column_row = row_of(R.ct)
     grads = R.gkv[...].reshape(LANDMARKS, WIN)
     stacked = jnp.concatenate([grads, R.wt[...]], axis=0)
-    for s in range(NS):
-        weight = R.wgt[s]
-        grad = (weight * (mm_t(R.kvx[s + 1], grads) - column_row)).astype(BF16)
-        R.dl[s] = grad
-        both = jnp.concatenate([weight.astype(BF16), grad], axis=1)
-        R.km[s] = (mm(both, stacked) + R.dkv[s + 1]).astype(BF16)
-        send_out(s, R.km, R.ki, R.k_s, R.k_r)
+    for s in every:
+        R.dl[s] = (R.wgt[s] * (mm_t(R.kvx[s + 1], grads) - column_row)).astype(BF16)
+    for first in range(0, NS, 4):
+        segs = range(first, min(first + 4, NS))
+        for s in segs:
+            both = jnp.concatenate([R.wgt[s].astype(BF16), R.dl[s]], axis=1)
+            R.km[s] = (mm(both, stacked) + R.dkv[s + 1]).astype(BF16)
+        for s in segs:
+            send_out(s, R.km, R.ki, R.k_s, R.k_r)
     proj = mm(R.kvt[:, WIN : (NS + 1) * WIN], R.dl[...].reshape(NS * WIN, LANDMARKS)).T
     LN = LANDMARKS // N
     norm_tile = functools.reduce(lambda a, b: a + b, [R.ct[p] for p in range(G)])
@@ -447,23 +461,31 @@
         rcopy(R.km.at[0], R.ki.at[h], R.k_s.at[0], R.k_r.at[h], (x, z, y, c)).wait_recv()
     for pair in range(Y // 2):
         cols = slice(pair * WIN, (pair + 1) * WIN)
-        R.gk_o[:, cols], R.gv_o[:, cols] = unpack_heads(R.ki[2 * pair], R.ki[2 * pair + 1])
+        R.gk_b[:, cols], R.gv_b[:, cols] = unpack_heads(R.ki[2 * pair], R.ki[2 * pair + 1])
+    store("gk", "gv")
     arrive(proj_copies)
     for h in range(Y):
-        R.gp_o[h] = R.pi[2 * h, 0:LN] + R.pi[2 * h + 1, 0:LN]
+        R.gp_b[h] = (R.pi[2 * h, 0:LN] + R.pi[2 * h + 1, 0:LN])[:, 0:DH]
     sums = functools.reduce(lambda a, b: a + b, [R.pi[2 * h, LN : LN + 8] for h in range(Y)])
-    R.gn_o[0:1] = sums[1:2, 0:DH]
-    R.gn_o[1:2] = sums[2:3, 0:DH]
-    R.gn_o[2:3] = sums[1:2, DH:]
-    R.gn_o[3:4] = sums[2:3, DH:]
-
-    sent_in(*kv_move)
-    sent_in(*qg_move)
-    for s in range(NS):
-        sent_out(s, R.om, R.oi, R.o_s, R.o_r)
-        sent_out(s, R.km, R.ki, R.k_s, R.k_r)
-    for copy in pending:
-        copy.wait_send()
+    R.gn_b[0:1] = sums[1:2, 0:DH]
+    R.gn_b[1:2] = sums[2:3, 0:DH]
+    R.gn_b[2:3] = sums[1:2, DH:]
+    R.gn_b[3:4] = sums[2:3, DH:]
+
+    store("gp", "gn")
+    for wait in unsent:
+        wait()
+    for copy in stores.values():
+        copy.wait()
+
+
+def store_kernel(*refs):
+    count = len(refs) // 2
+    copies = [pltpu.make_async_copy(refs[i], refs[count + i], refs[-1].at[i]) for i in range(count)]
+    for copy in copies:
+        copy.start()
+    for copy in copies:
+        copy.wait()
 
 
 def layer(dims, q, k, v, w, gain, bias, g):
@@ -472,7 +494,15 @@
     CH, LN = LANDMARKS // G, LANDMARKS // N
     block = (WIN, WIN)
     dma = pltpu.SemaphoreType.DMA
+    tokens = ((WIN, Y * DH), BF16)
     scratch = dict(
+        q=tokens,
+        k=tokens,
+        v=tokens,
+        g=tokens,
+        w=((DH, LANDMARKS), BF16),
+        gain=((2, DH), F32),
+        bias=((2, DH), F32),
         kvm=((Y, *block), BF16),
         qgm=((Y, *block), BF16),
         kvx=((NS + 2, *block), BF16),
@@ -517,26 +547,36 @@
         d=2, o=Y, k=Y, p=N - 1,
     )
     sems = {f"{name}_{side}": dma((count,)) for name, count in counts.items() for side in "sr"}
+    sems["in_s"] = dma((7,))
     outs = dict(
-        att_o=((WIN, Y * DH), BF16),
-        gq_o=((WIN, Y * DH), BF16),
-        gk_o=((WIN, Y * DH), BF16),
-        gv_o=((WIN, Y * DH), BF16),
-        gp_o=((Y, LN, WIN), F32),
+        att_o=tokens,
+        gq_o=tokens,
+        gk_o=tokens,
+        gv_o=tokens,
+        gp_o=((Y, LN, DH), F32),
         gn_o=((4, DH), F32),
     )
-    names = ("q", "k", "v", "w", "gain", "bias", "g", *outs, *scratch, *sems)
-    att, gq, gk, gv, gp, gn = pl.pallas_call(
+    scratch.update({name[:-2] + "_b": o for name, o in outs.items()})
+    sems["out_s"] = dma((len(outs),))
+    names = ("q_i", "k_i", "v_i", "w_i", "gain_i", "bias_i", "g_i", *outs, *scratch, *sems)
+    results = pl.pallas_call(
         functools.partial(kernel, dims, names),
         out_shape=[jax.ShapeDtypeStruct(*o) for o in outs.values()],
-        in_specs=[pl.BlockSpec(memory_space=pltpu.VMEM)] * 7,
-        out_specs=[pl.BlockSpec(memory_space=pltpu.VMEM)] * len(outs),
+        in_specs=[pl.BlockSpec(memory_space=pl.ANY)] * 7,
+        out_specs=[pl.BlockSpec(memory_space=pl.ANY)] * len(outs),
         scratch_shapes=[pltpu.VMEM(*s) for s in scratch.values()] + list(sems.values()),
         compiler_params=pltpu.CompilerParams(
-            collective_id=0, has_side_effects=True, vmem_limit_bytes=40 * 1024 * 1024
+            collective_id=0, has_side_effects=True, vmem_limit_bytes=60 * 1024 * 1024
         ),
     )(q, k, v, w, gain, bias, g)
-    return att, gq, gk, gv, gp[:, :, :DH].transpose(0, 2, 1)[None], gn
+    att, gq, gk, gv, gp, gn = pl.pallas_call(
+        store_kernel,
+        out_shape=[jax.ShapeDtypeStruct(*o) for o in outs.values()],
+        in_specs=[pl.BlockSpec(memory_space=pl.ANY)] * len(outs),
+        out_specs=[pl.BlockSpec(memory_space=pl.ANY)] * len(outs),
+        scratch_shapes=[dma((len(outs),))],
+    )(*results)
+    return att, gq, gk, gv, gp.transpose(0, 2, 1)[None], gn
 
 
 def build(devices):

time: 83.3 us -> 90.9 us (1.091)
  Pallas kernels: 72.7 us -> 90.1 us
  local copies, waits for them, and re-layouts: 9.75 us -> 0 us
    pallas_call x0 -> x1, Pallas kernels: none -> 19.1 us  [layer(): pl.pallas_call(store_kernel, out_shape=[jax.ShapeDtypeStruct(*o) for o in...]
    unnamed x19 -> x0, local copies, waits for them, and re-layouts: 9.11 us -> none
    pallas_call x1, Pallas kernels: 72.7 us -> 71.1 us  [layer(): pl.pallas_call(functools.partial(kernel, dims, names), out_shape=[jax.Sha...]
where the time goes in v2:
time: 90.9 us; the launch traced here: 90.8 us
  Pallas kernels  90.1 us (99%)
    pallas_call x1, Pallas kernels, layer(): pl.pallas_call(functools.partial(kernel, dims, names), out_shape=[jax.Sha...  71.1 us
    pallas_call x1, Pallas kernels, layer(): pl.pallas_call(store_kernel, out_shape=[jax.ShapeDtypeStruct(*o) for o in...  19.1 us

profile of v2, /device:TPU:1, one launch (start us, length us, event | category | flops | bytes accessed | tf_op | source)
XLA Modules:
  0.0 90.8 jit_solution(6007034521991888325)
XLA Ops:
  0.6 71.1 %shard_map.118 = (bf16[128,512]{1,0:T(8,128)(2,1)}, bf16[128,512]{1,0:T(8,128)(2,1)}, bf16[128,512]{1,0:T(8,128)(2,1)}, bf16[128,512]{1,0:T(8,128)(2,1)}, f32[8,16,64]{2,1,0:T(8,128)}, /*index=5*/f32[4,64]{1,0:T(4,128)}) custom-call(bf16[128,512]{1,0:T(8,128)(2,1)} %refs_0_.1, bf16[128,512]{1,0:T(8,128)(2,1)} %refs_1_.1, bf16[128,512]{1,0:T(8,128)(2,1)} %refs_2_.1, ...), custom_call_target="tpu_custom_call" | custom-call | tf_op jit(solution)/shard_map/pallas_call | solution.py:562
  71.7 19.1 %shard_map.119 = (bf16[128,512]{1,0:T(8,128)(2,1)}, bf16[128,512]{1,0:T(8,128)(2,1)}, bf16[128,512]{1,0:T(8,128)(2,1)}, bf16[128,512]{1,0:T(8,128)(2,1)}, f32[8,16,64]{2,1,0:T(8,128)}, /*index=5*/f32[4,64]{1,0:T(4,128)}) custom-call(bf16[128,512]{1,0:T(8,128)(2,1)} %get-tuple-element.18.refs_0_, bf16[128,512]{1,0:T(8,128)(2,1)} %get-tuple-element.19.refs_1_, ...), custom_call_target="tpu_custom_call" | custom-call | tf_op jit(solution)/shard_map/pallas_call | solution.py:572

commit v3 on v2

--- a/solution.py
+++ b/solution.py
@@ -34,6 +34,10 @@
 
 def mm_t(a, b):
     return lax.dot_general(a, b, (((1,), (1,)), ((), ())), preferred_element_type=F32)
+
+
+def far_first(size):
+    return sorted(range(1, size), key=lambda o: -min(o, size - o))
 
 
 def left_half(shape):
@@ -161,7 +165,7 @@
     self_in = c == core_in
 
     def send_in(src, dst, base, send, recv):
-        for o in range(Y):
+        for o in (*far_first(Y), 0):
             to = lax.rem(y + o, Y)
             remote = rcopy(src.at[to], dst.at[base + slot_in], send.at[o], recv.at[slot_in], (x, z, to, core_in))
             if o:
@@ -213,15 +217,15 @@
     def scatter_copies(src, dst, send, recv):
         return [
             rcopy(src.at[lax.rem(r + o, G)], dst.at[o - 1], send.at[o - 1], recv.at[o - 1], plane_dev(o))
-            for o in range(1, G)
+            for o in far_first(G)
         ]
 
     def z_copies(src, dst, send, recv):
-        return [rcopy(src, dst.at[o - 1], send.at[o - 1], recv.at[o - 1], z_dev(o)) for o in range(1, Z)]
+        return [rcopy(src, dst.at[o - 1], send.at[o - 1], recv.at[o - 1], z_dev(o)) for o in far_first(Z)]
 
     def gather_copies(buf, send, recv):
         return [
-            rcopy(buf.at[r], buf.at[r], send.at[o - 1], recv.at[o - 1], plane_dev(o)) for o in range(1, G)
+            rcopy(buf.at[r], buf.at[r], send.at[o - 1], recv.at[o - 1], plane_dev(o)) for o in far_first(G)
         ]
 
     def start(copies):
@@ -271,8 +275,6 @@
             zero = jnp.zeros_like(qg)
             R.rr[s, 0:WIN] = jnp.where(left, qg * jnp.asarray(0.125, BF16), zero)
             R.rr[s, WIN : 2 * WIN] = jnp.where(left, zero, qg)
-        for s in segs:
-            R.gt[s] = R.qg[s].astype(F32).T[DH:]
         for s in segs:
             both = mm_t(R.kvx[s : s + 3].reshape(3 * WIN, WIN), R.rr[s])
             scores = both[:, 0:WIN]
@@ -288,8 +290,9 @@
         weights = {}
         for s in segs:
             weight = jnp.exp(R.sw[s] - tops[s])
-            R.mw[s] = jnp.broadcast_to(tops[s], (8, WIN))
-            R.lw[s] = jnp.broadcast_to(jnp.sum(weight, axis=0, keepdims=True), (8, WIN))
+            R.mw[s, 0:1] = tops[s]
+            R.lw[s, 0:1] = jnp.sum(weight, axis=0, keepdims=True)
+            R.dw[s, 0:1] = jnp.sum(weight * R.gpw[s], axis=0, keepdims=True)
             weights[s] = weight.astype(BF16)
         for s in segs:
             R.ow[s] = mm(R.kvt[:, s * WIN : (s + 3) * WIN], weights[s])
@@ -315,8 +318,6 @@
     arrive(gather_1)
 
     land = R.land[...].reshape(LANDMARKS, WIN)
-    land_t = land.astype(F32).T.astype(BF16)
-    R.landt[...] = land_t
     every = range(NS)
     both = [mm_t(land, R.rr[s]) for s in every]
     tops = [jnp.maximum(R.mw[s, 0:1], jnp.max(both[s][:, 0:WIN], axis=0, keepdims=True)) for s in every]
@@ -325,19 +326,22 @@
     totals = [R.lw[s, 0:1] * shrinks[s] + jnp.sum(weights[s], axis=0, keepdims=True) for s in every]
     pers = [1.0 / t for t in totals]
     probs = [w * per for w, per in zip(weights, pers)]
+    deltas = [
+        (R.dw[s, 0:1] * shrinks[s] + jnp.sum(weights[s] * both[s][:, WIN:], axis=0, keepdims=True)) * pers[s]
+        for s in every
+    ]
     for s in every:
         R.dp[:, (2 * s + 1) * WIN : (2 * s + 2) * WIN] = probs[s].astype(BF16)
-        R.mw[s] = jnp.broadcast_to(tops[s] + jnp.log(totals[s]), (8, WIN))
+        R.dp[:, 2 * s * WIN : (2 * s + 1) * WIN] = (probs[s] * (both[s][:, WIN:] - deltas[s])).astype(BF16)
     for s in every:
-        R.ow[s] = R.ow[s] * (shrinks[s] * pers[s]) + mm(land_t, R.dp[:, (2 * s + 1) * WIN : (2 * s + 2) * WIN])
-    deltas = [jnp.sum(R.ow[s, DH:] * R.gt[s], axis=0, keepdims=True) for s in every]
-    for s in every:
-        R.dp[:, 2 * s * WIN : (2 * s + 1) * WIN] = (probs[s] * (both[s][:, WIN:] - deltas[s])).astype(BF16)
-        R.lw[s] = jnp.broadcast_to(deltas[s], (8, WIN))
+        R.mw[s, 0:1] = tops[s] + jnp.log(totals[s])
+        R.lw[s, 0:1] = deltas[s]
+        R.cf[s, 0:1] = shrinks[s] * pers[s]
     R.s3[...] = mm(R.dp[...], R.rr[...].reshape(2 * NS * WIN, WIN)).reshape(G, CH, WIN)
     scatter_2 = start(scatter_copies(R.s3, R.r3, R.s3_s, R.s3_r))
 
     R.dkv[...] = jnp.zeros_like(R.dkv)
+    R.landt[...] = land.astype(F32).T.astype(BF16)
 
     def is_own(s):
         return n == c * NS + s
@@ -368,7 +372,8 @@
             grad_q = mm(R.kvt[:, s * WIN : (s + 3) * WIN], grads[s]) + mm(
                 R.landt[...], R.dp[:, 2 * s * WIN : (2 * s + 1) * WIN]
             )
-            packed.append(jnp.where(rows, grad_q * 0.125, R.ow[s]))
+            out_t = R.ow[s] * R.cf[s, 0:1] + mm(R.landt[...], R.dp[:, (2 * s + 1) * WIN : (2 * s + 2) * WIN])
+            packed.append(jnp.where(rows, grad_q * 0.125, out_t))
         for s, block in zip(segs, packed):
             R.om[s] = block.T.astype(BF16)
         for s in segs:
@@ -418,7 +423,9 @@
     arrive(gather_l)
     log_row = row_of(R.lt)
     for s in range(NS):
-        R.wgt[s] = jnp.exp(mm(R.kvx[s + 1], R.wp[...]) - log_row)
+        weight = jnp.exp(mm(R.kvx[s + 1], R.wp[...]) - log_row)
+        R.wgt[s] = weight
+        R.wgb[s] = weight.astype(BF16)
     arrive(back)
     R.dkv[1] += R.dh[0]
     R.dkv[NS] += R.dh[1]
@@ -434,26 +441,30 @@
     arrive(gather_c)
     column_row = row_of(R.ct)
     grads = R.gkv[...].reshape(LANDMARKS, WIN)
-    stacked = jnp.concatenate([grads, R.wt[...]], axis=0)
     for s in every:
         R.dl[s] = (R.wgt[s] * (mm_t(R.kvx[s + 1], grads) - column_row)).astype(BF16)
+    R.nt[y] = functools.reduce(lambda a, b: a + b, [R.ct[p] for p in range(G)])
+    norm_copies = start(
+        [
+            rcopy(R.nt.at[y], R.nt.at[y], R.n_s.at[o - 1], R.n_r.at[o - 1], (x, z, lax.rem(y + o, Y), c))
+            for o in far_first(Y)
+        ]
+    )
     for first in range(0, NS, 4):
         segs = range(first, min(first + 4, NS))
         for s in segs:
-            both = jnp.concatenate([R.wgt[s].astype(BF16), R.dl[s]], axis=1)
-            R.km[s] = (mm(both, stacked) + R.dkv[s + 1]).astype(BF16)
+            R.km[s] = (mm(R.wgb[s], grads) + mm(R.dl[s], R.wt[...]) + R.dkv[s + 1]).astype(BF16)
         for s in segs:
             send_out(s, R.km, R.ki, R.k_s, R.k_r)
     proj = mm(R.kvt[:, WIN : (NS + 1) * WIN], R.dl[...].reshape(NS * WIN, LANDMARKS)).T
-    LN = LANDMARKS // N
-    norm_tile = functools.reduce(lambda a, b: a + b, [R.ct[p] for p in range(G)])
-    for m in range(N):
-        R.pm[m, 0:LN] = proj[m * LN : (m + 1) * LN]
-        R.pm[m, LN : LN + 8] = norm_tile
+    HN = LANDMARKS // N // 2
+    halves = proj.reshape(N, 2, HN, WIN)
+    low, high = halves[:, 0].reshape(N * HN, WIN), halves[:, 1].reshape(N * HN, WIN)
+    R.pm[...] = jnp.where(left_half(low.shape), low, pltpu.roll(high, DH, 1)).reshape(N, HN, WIN)
     proj_copies = start(
         [
             rcopy(R.pm.at[lax.rem(n + o, N)], R.pi.at[n], R.p_s.at[o - 1], R.p_r.at[o - 1], inner_dev(lax.rem(n + o, N)))
-            for o in range(1, N)
+            for o in far_first(N)
         ]
     )
     R.pi[n] = R.pm[n]
@@ -465,8 +476,11 @@
     store("gk", "gv")
     arrive(proj_copies)
     for h in range(Y):
-        R.gp_b[h] = (R.pi[2 * h, 0:LN] + R.pi[2 * h + 1, 0:LN])[:, 0:DH]
-    sums = functools.reduce(lambda a, b: a + b, [R.pi[2 * h, LN : LN + 8] for h in range(Y)])
+        both = R.pi[2 * h] + R.pi[2 * h + 1]
+        R.gp_b[h, 0:HN] = both[:, 0:DH]
+        R.gp_b[h, HN : 2 * HN] = pltpu.roll(both, DH, 1)[:, 0:DH]
+    arrive(norm_copies)
+    sums = functools.reduce(lambda a, b: a + b, [R.nt[h] for h in range(Y)])
     R.gn_b[0:1] = sums[1:2, 0:DH]
     R.gn_b[1:2] = sums[2:3, 0:DH]
     R.gn_b[2:3] = sums[1:2, DH:]
@@ -479,12 +493,17 @@
         copy.wait()
 
 
-def store_kernel(*refs):
-    count = len(refs) // 2
-    copies = [pltpu.make_async_copy(refs[i], refs[count + i], refs[-1].at[i]) for i in range(count)]
-    for copy in copies:
+def store_kernel(count, *refs):
+    src, dst, via = (refs[i * count : (i + 1) * count] for i in range(3))
+    read, written = refs[3 * count :]
+    reads = [pltpu.make_async_copy(src[i], via[i], read.at[i]) for i in range(count)]
+    writes = [pltpu.make_async_copy(via[i], dst[i], written.at[i]) for i in range(count)]
+    for copy in reads:
         copy.start()
-    for copy in copies:
+    for before, after in zip(reads, writes):
+        before.wait()
+        after.start()
+    for copy in writes:
         copy.wait()
 
 
@@ -515,7 +534,8 @@
         r2=((Z - 1, CH + 8, WIN), F32),
         kvt=((WIN, (NS + 2) * WIN), BF16),
         rr=((NS, 2 * WIN, WIN), BF16),
-        gt=((NS, DH, WIN), F32),
+        dw=((NS, 8, WIN), F32),
+        cf=((NS, 8, WIN), F32),
         sw=((NS, 3 * WIN, WIN), F32),
         gpw=((NS, 3 * WIN, WIN), F32),
         mw=((NS, 8, WIN), F32),
@@ -536,15 +556,17 @@
         gkv=((G, CH, WIN), BF16),
         ct=((G, 8, WIN), F32),
         wgt=((NS, WIN, LANDMARKS), F32),
+        wgb=((NS, WIN, LANDMARKS), BF16),
         dl=((NS, WIN, LANDMARKS), BF16),
         km=((NS, *block), BF16),
         ki=((Y, *block), BF16),
-        pm=((N, LN + 8, WIN), F32),
-        pi=((N, LN + 8, WIN), F32),
+        pm=((N, LN // 2, WIN), F32),
+        pi=((N, LN // 2, WIN), F32),
+        nt=((Y, 8, WIN), F32),
     )
     counts = dict(
         kv=Y, qg=Y, h=2, s1=G - 1, s2=Z - 1, g1=G - 1, gl=G - 1, s3=G - 1, s4=Z - 1, g2=G - 1, gc=G - 1,
-        d=2, o=Y, k=Y, p=N - 1,
+        d=2, o=Y, k=Y, p=N - 1, n=Y - 1,
     )
     sems = {f"{name}_{side}": dma((count,)) for name, count in counts.items() for side in "sr"}
     sems["in_s"] = dma((7,))
@@ -570,11 +592,11 @@
         ),
     )(q, k, v, w, gain, bias, g)
     att, gq, gk, gv, gp, gn = pl.pallas_call(
-        store_kernel,
+        functools.partial(store_kernel, len(outs)),
         out_shape=[jax.ShapeDtypeStruct(*o) for o in outs.values()],
         in_specs=[pl.BlockSpec(memory_space=pl.ANY)] * len(outs),
         out_specs=[pl.BlockSpec(memory_space=pl.ANY)] * len(outs),
-        scratch_shapes=[dma((len(outs),))],
+        scratch_shapes=[pltpu.VMEM(*o) for o in outs.values()] + [dma((len(outs),))] * 2,
     )(*results)
     return att, gq, gk, gv, gp.transpose(0, 2, 1)[None], gn
 

time: 90.9 us -> 70.4 us (0.77)
  Pallas kernels: 90.1 us -> 69.6 us
    pallas_call x1, Pallas kernels: 19.1 us -> 1.87 us  [layer(): pl.pallas_call(functools.partial(store_kernel, len(outs)), out_shape=[jax...]
    pallas_call x1, Pallas kernels: 71.1 us -> 67.7 us  [layer(): pl.pallas_call(functools.partial(kernel, dims, names), out_shape=[jax.Sha...]
where the time goes in v3:
time: 70.4 us; the launch traced here: 70.3 us
  Pallas kernels  69.6 us (99%)
    pallas_call x1, Pallas kernels, layer(): pl.pallas_call(functools.partial(kernel, dims, names), out_shape=[jax.Sha...  67.7 us
    pallas_call x1, Pallas kernels, layer(): pl.pallas_call(functools.partial(store_kernel, len(outs)), out_shape=[jax...  1.87 us

profile of v3, /device:TPU:1, one launch (start us, length us, event | category | flops | bytes accessed | tf_op | source)
XLA Modules:
  0.0 70.3 jit_solution(4187117648769314250)
XLA Ops:
  0.6 67.7 %shard_map.118 = (bf16[128,512]{1,0:T(8,128)(2,1)}, bf16[128,512]{1,0:T(8,128)(2,1)}, bf16[128,512]{1,0:T(8,128)(2,1)}, bf16[128,512]{1,0:T(8,128)(2,1)}, f32[8,16,64]{2,1,0:T(8,128)}, /*index=5*/f32[4,64]{1,0:T(4,128)}) custom-call(bf16[128,512]{1,0:T(8,128)(2,1)} %refs_0_.1, bf16[128,512]{1,0:T(8,128)(2,1)} %refs_1_.1, bf16[128,512]{1,0:T(8,128)(2,1)} %refs_2_.1, ...), custom_call_target="tpu_custom_call" | custom-call | tf_op jit(solution)/shard_map/pallas_call | solution.py:584
  68.4 1.9 %shard_map.119 = (bf16[128,512]{1,0:T(8,128)(2,1)}, bf16[128,512]{1,0:T(8,128)(2,1)}, bf16[128,512]{1,0:T(8,128)(2,1)}, bf16[128,512]{1,0:T(8,128)(2,1)}, f32[8,16,64]{2,1,0:T(8,128)}, /*index=5*/f32[4,64]{1,0:T(4,128)}) custom-call(bf16[128,512]{1,0:T(8,128)(2,1)} %get-tuple-element.18.refs_0_, bf16[128,512]{1,0:T(8,128)(2,1)} %get-tuple-element.19.refs_1_, ...), custom_call_target="tpu_custom_call" | custom-call | tf_op jit(solution)/shard_map/pallas_call | solution.py:594

commit v4 on v3

--- a/solution.py
+++ b/solution.py
@@ -80,12 +80,27 @@
     return jnp.sum(jnp.where(diag, row, 0.0), axis=1, keepdims=True)
 
 
-def combine(parts):
-    peak = functools.reduce(jnp.maximum, [log_weight for _, log_weight in parts])
-    scaled = [(mean, jnp.exp(log_weight - peak)) for mean, log_weight in parts]
-    total = functools.reduce(lambda a, b: a + b, [w for _, w in scaled])
-    mean = functools.reduce(lambda a, b: a + b, [m * w for m, w in scaled])
-    return mean / total, peak + jnp.log(total)
+def split_row(row, rows):
+    pieces = []
+    rest = row
+    for _ in range(3):
+        pieces.append(rest.astype(BF16).astype(F32))
+        rest = rest - pieces[-1]
+    return jnp.concatenate([*pieces, jnp.zeros((rows - 3, row.shape[1]), F32)], axis=0).astype(BF16)
+
+
+def join_rows(block):
+    block = block.astype(F32)
+    return block[0:1] + (block[1:2] + block[2:3])
+
+
+def combine(parts, n):
+    peak = functools.reduce(jnp.maximum, [row for _, row in parts])
+    weights = [jnp.exp(row - peak) for _, row in parts]
+    total = functools.reduce(lambda a, b: a + b, weights)
+    per = 1.0 / total
+    scaled = [mean.astype(F32) * as_col(w * per, n, 0) for (mean, _), w in zip(parts, weights)]
+    return functools.reduce(lambda a, b: a + b, scaled), peak + jnp.log(total)
 
 
 def kernel(dims, names, *refs):
@@ -211,8 +226,8 @@
     log_weights = peak + jnp.log(total)
     for p in range(G):
         rows = slice(p * CH, (p + 1) * CH)
-        R.s1[p, 0:CH] = means[rows]
-        R.s1[p, CH : CH + 8] = jnp.broadcast_to(as_row(log_weights[rows], 0), (8, WIN))
+        R.s1[p, 0:CH] = means[rows].astype(BF16)
+        R.s1[p, CH : CH + 16] = split_row(as_row(log_weights[rows], 0), 16)
 
     def scatter_copies(src, dst, send, recv):
         return [
@@ -254,12 +269,12 @@
         transpose_kv(s)
 
     def part_of(ref, o):
-        return (ref[o, 0:CH], as_col(ref[o, CH : CH + 1], CH, 0))
+        return (ref[o, 0:CH], join_rows(ref[o, CH : CH + 16]))
 
     arrive(scatter_1)
-    mean, log_weight = combine([part_of(R.s1, r)] + [part_of(R.r1, o) for o in range(G - 1)])
-    R.s2[0:CH] = mean
-    R.s2[CH : CH + 8] = jnp.broadcast_to(as_row(log_weight, 0), (8, WIN))
+    mean, log_weight = combine([part_of(R.s1, r)] + [part_of(R.r1, o) for o in range(G - 1)], CH)
+    R.s2[0:CH] = mean.astype(BF16)
+    R.s2[CH : CH + 16] = split_row(log_weight, 16)
     z_1 = start(z_copies(R.s2, R.r2, R.s2_s, R.s2_r))
 
     arrive(halo)
@@ -302,7 +317,7 @@
 
     arrive(z_1)
     mean, log_weight = combine(
-        [(mean, log_weight)] + [part_of(R.r2, o) for o in range(Z - 1)]
+        [(R.s2[0:CH], log_weight)] + [part_of(R.r2, o) for o in range(Z - 1)], CH
     )
     centred = mean - half_mean(mean)
     inverse = 1.0 / jnp.sqrt(half_mean(centred * centred) + 1e-05)
@@ -310,7 +325,7 @@
     R.land[r] = (normed * gain + bias).astype(BF16)
     gather_1 = start(gather_copies(R.land, R.g1_s, R.g1_r))
     base = lax.rem(r * CH, WIN)
-    R.lt[r] = jnp.broadcast_to(as_row(log_weight, base), (8, WIN))
+    R.lt[r] = jnp.broadcast_to(as_row(as_col(log_weight, CH, 0), base), (8, WIN))
     gather_l = start(gather_copies(R.lt, R.gl_s, R.gl_r))
 
     window_scores(range(split, NS))
@@ -337,7 +352,7 @@
         R.mw[s, 0:1] = tops[s] + jnp.log(totals[s])
         R.lw[s, 0:1] = deltas[s]
         R.cf[s, 0:1] = shrinks[s] * pers[s]
-    R.s3[...] = mm(R.dp[...], R.rr[...].reshape(2 * NS * WIN, WIN)).reshape(G, CH, WIN)
+    R.s3[...] = mm(R.dp[...], R.rr[...].reshape(2 * NS * WIN, WIN)).astype(BF16).reshape(G, CH, WIN)
     scatter_2 = start(scatter_copies(R.s3, R.r3, R.s3_s, R.s3_r))
 
     R.dkv[...] = jnp.zeros_like(R.dkv)
@@ -381,10 +396,10 @@
 
     window_grads(range(split))
     arrive(scatter_2)
-    land_grad = R.s3[r]
+    land_grad = R.s3[r].astype(F32)
     for o in range(G - 1):
-        land_grad = land_grad + R.r3[o]
-    R.s4[...] = land_grad
+        land_grad = land_grad + R.r3[o].astype(F32)
+    R.s4[...] = land_grad.astype(BF16)
     z_2 = start(z_copies(R.s4, R.r4, R.s4_s, R.s4_r))
     window_grads(range(split, NS))
     back = start(
@@ -394,34 +409,36 @@
         ]
     )
     arrive(z_2)
+    land_grad = R.s4[...].astype(F32)
     for o in range(Z - 1):
-        land_grad = land_grad + R.r4[o]
+        land_grad = land_grad + R.r4[o].astype(F32)
     scaled = land_grad * gain
     grad_mean = inverse * (scaled - half_mean(scaled) - normed * half_mean(scaled * normed))
     grad_mean_b = grad_mean.astype(BF16)
-    R.gkv[r] = grad_mean_b
+    column = jnp.sum(grad_mean_b.astype(F32) * mean, axis=1, keepdims=True)
+    R.gkv[r, 0:CH] = grad_mean_b
+    R.gkv[r, CH : CH + 16] = split_row(as_row(column, base), 16)
     gather_2 = start(gather_copies(R.gkv, R.g2_s, R.g2_r))
-    column = jnp.sum(grad_mean_b.astype(F32) * mean, axis=1, keepdims=True)
     R.ct[r] = jnp.concatenate(
         [
-            as_row(column, base),
             jnp.sum(land_grad * normed, axis=0, keepdims=True),
             jnp.sum(land_grad, axis=0, keepdims=True),
-            jnp.zeros((5, WIN), F32),
+            jnp.zeros((6, WIN), F32),
         ],
         axis=0,
     )
     gather_c = start(gather_copies(R.ct, R.gc_s, R.gc_r))
 
-    def row_of(ref):
+    def row_of(pieces):
         per = WIN // CH
-        rows = []
-        for first in range(0, G, per):
-            rows.append(functools.reduce(lambda a, b: a + b, [ref[p, 0:1] for p in range(first, first + per)]))
+        rows = [
+            functools.reduce(lambda a, b: a + b, [pieces[p] for p in range(first, first + per)])
+            for first in range(0, G, per)
+        ]
         return jnp.concatenate(rows, axis=1)
 
     arrive(gather_l)
-    log_row = row_of(R.lt)
+    log_row = row_of([R.lt[p, 0:1] for p in range(G)])
     for s in range(NS):
         weight = jnp.exp(mm(R.kvx[s + 1], R.wp[...]) - log_row)
         R.wgt[s] = weight
@@ -438,11 +455,22 @@
     store("gq", "att")
 
     arrive(gather_2)
-    arrive(gather_c)
-    column_row = row_of(R.ct)
-    grads = R.gkv[...].reshape(LANDMARKS, WIN)
+    column_row = row_of([join_rows(R.gkv[p, CH : CH + 16]) for p in range(G)])
+    grads = R.gkv[:, 0:CH].reshape(LANDMARKS, WIN)
     for s in every:
         R.dl[s] = (R.wgt[s] * (mm_t(R.kvx[s + 1], grads) - column_row)).astype(BF16)
+
+    turn = lax.rem(y, half) + jnp.where(core_in == c, 0, half // 2)
+    segs = [2 * lax.rem(turn + o, half) + i for o in (*far_first(half), 0) for i in range(2)]
+
+    def send_kv_grads(segs):
+        for s in segs:
+            R.km[s] = (mm(R.wgb[s], grads) + mm(R.dl[s], R.wt[...]) + R.dkv[s + 1]).astype(BF16)
+        for s in segs:
+            send_out(s, R.km, R.ki, R.k_s, R.k_r)
+
+    send_kv_grads(segs[: NS // 2])
+    arrive(gather_c)
     R.nt[y] = functools.reduce(lambda a, b: a + b, [R.ct[p] for p in range(G)])
     norm_copies = start(
         [
@@ -450,12 +478,6 @@
             for o in far_first(Y)
         ]
     )
-    for first in range(0, NS, 4):
-        segs = range(first, min(first + 4, NS))
-        for s in segs:
-            R.km[s] = (mm(R.wgb[s], grads) + mm(R.dl[s], R.wt[...]) + R.dkv[s + 1]).astype(BF16)
-        for s in segs:
-            send_out(s, R.km, R.ki, R.k_s, R.k_r)
     proj = mm(R.kvt[:, WIN : (NS + 1) * WIN], R.dl[...].reshape(NS * WIN, LANDMARKS)).T
     HN = LANDMARKS // N // 2
     halves = proj.reshape(N, 2, HN, WIN)
@@ -468,6 +490,7 @@
         ]
     )
     R.pi[n] = R.pm[n]
+    send_kv_grads(segs[NS // 2 :])
     for h in range(Y):
         rcopy(R.km.at[0], R.ki.at[h], R.k_s.at[0], R.k_r.at[h], (x, z, y, c)).wait_recv()
     for pair in range(Y // 2):
@@ -481,10 +504,10 @@
         R.gp_b[h, HN : 2 * HN] = pltpu.roll(both, DH, 1)[:, 0:DH]
     arrive(norm_copies)
     sums = functools.reduce(lambda a, b: a + b, [R.nt[h] for h in range(Y)])
-    R.gn_b[0:1] = sums[1:2, 0:DH]
-    R.gn_b[1:2] = sums[2:3, 0:DH]
-    R.gn_b[2:3] = sums[1:2, DH:]
-    R.gn_b[3:4] = sums[2:3, DH:]
+    R.gn_b[0:1] = sums[0:1, 0:DH]
+    R.gn_b[1:2] = sums[1:2, 0:DH]
+    R.gn_b[2:3] = sums[0:1, DH:]
+    R.gn_b[3:4] = sums[1:2, DH:]
 
     store("gp", "gn")
     for wait in unsent:
@@ -528,10 +551,10 @@
         qg=((NS, *block), BF16),
         wp=((WIN, LANDMARKS), BF16),
         wt=((LANDMARKS, WIN), BF16),
-        s1=((G, CH + 8, WIN), F32),
-        r1=((G - 1, CH + 8, WIN), F32),
-        s2=((CH + 8, WIN), F32),
-        r2=((Z - 1, CH + 8, WIN), F32),
+        s1=((G, CH + 16, WIN), BF16),
+        r1=((G - 1, CH + 16, WIN), BF16),
+        s2=((CH + 16, WIN), BF16),
+        r2=((Z - 1, CH + 16, WIN), BF16),
         kvt=((WIN, (NS + 2) * WIN), BF16),
         rr=((NS, 2 * WIN, WIN), BF16),
         dw=((NS, 8, WIN), F32),
@@ -545,15 +568,15 @@
         lt=((G, 8, WIN), F32),
         landt=((WIN, LANDMARKS), BF16),
         dp=((LANDMARKS, 2 * NS * WIN), BF16),
-        s3=((G, CH, WIN), F32),
-        r3=((G - 1, CH, WIN), F32),
-        s4=((CH, WIN), F32),
-        r4=((Z - 1, CH, WIN), F32),
+        s3=((G, CH, WIN), BF16),
+        r3=((G - 1, CH, WIN), BF16),
+        s4=((CH, WIN), BF16),
+        r4=((Z - 1, CH, WIN), BF16),
         dkv=((NS + 2, *block), F32),
         dh=((2, *block), F32),
         om=((NS, *block), BF16),
         oi=((Y, *block), BF16),
-        gkv=((G, CH, WIN), BF16),
+        gkv=((G, CH + 16, WIN), BF16),
         ct=((G, 8, WIN), F32),
         wgt=((NS, WIN, LANDMARKS), F32),
         wgb=((NS, WIN, LANDMARKS), BF16),

time: 70.4 us -> 68.1 us (0.967)
  Pallas kernels: 69.6 us -> 67.3 us
    pallas_call x1, Pallas kernels: 67.7 us -> 65.4 us  [layer(): pl.pallas_call(functools.partial(kernel, dims, names), out_shape=[jax.Sha...]
where the time goes in v4:
time: 68.1 us; the launch traced here: 67.9 us
  Pallas kernels  67.3 us (99%)
    pallas_call x1, Pallas kernels, layer(): pl.pallas_call(functools.partial(kernel, dims, names), out_shape=[jax.Sha...  65.4 us
    pallas_call x1, Pallas kernels, layer(): pl.pallas_call(functools.partial(store_kernel, len(outs)), out_shape=[jax...  1.87 us

profile of v4, /device:TPU:1, one launch (start us, length us, event | category | flops | bytes accessed | tf_op | source)
XLA Modules:
  0.0 67.9 jit_solution(2682574164159755635)
XLA Ops:
  0.6 65.4 %shard_map.118 = (bf16[128,512]{1,0:T(8,128)(2,1)}, bf16[128,512]{1,0:T(8,128)(2,1)}, bf16[128,512]{1,0:T(8,128)(2,1)}, bf16[128,512]{1,0:T(8,128)(2,1)}, f32[8,16,64]{2,1,0:T(8,128)}, /*index=5*/f32[4,64]{1,0:T(4,128)}) custom-call(bf16[128,512]{1,0:T(8,128)(2,1)} %refs_0_.1, bf16[128,512]{1,0:T(8,128)(2,1)} %refs_1_.1, bf16[128,512]{1,0:T(8,128)(2,1)} %refs_2_.1, ...), custom_call_target="tpu_custom_call" | custom-call | tf_op jit(solution)/shard_map/pallas_call | solution.py:607
  66.0 1.9 %shard_map.119 = (bf16[128,512]{1,0:T(8,128)(2,1)}, bf16[128,512]{1,0:T(8,128)(2,1)}, bf16[128,512]{1,0:T(8,128)(2,1)}, bf16[128,512]{1,0:T(8,128)(2,1)}, f32[8,16,64]{2,1,0:T(8,128)}, /*index=5*/f32[4,64]{1,0:T(4,128)}) custom-call(bf16[128,512]{1,0:T(8,128)(2,1)} %get-tuple-element.18.refs_0_, bf16[128,512]{1,0:T(8,128)(2,1)} %get-tuple-element.19.refs_1_, ...), custom_call_target="tpu_custom_call" | custom-call | tf_op jit(solution)/shard_map/pallas_call | solution.py:617

commit v5 on v4

--- a/solution.py
+++ b/solution.py
@@ -217,18 +217,6 @@
     for j in range(NS):
         received(*kv_move, j)
 
-    kv_own = R.kvx[1 : NS + 1].reshape(NS * WIN, WIN)
-    logits = mm_t(R.wt[...], kv_own)
-    peak = jnp.max(logits, axis=1, keepdims=True)
-    expo = jnp.exp(logits - peak)
-    total = jnp.sum(expo, axis=1, keepdims=True)
-    means = mm(expo.astype(BF16), kv_own) / total
-    log_weights = peak + jnp.log(total)
-    for p in range(G):
-        rows = slice(p * CH, (p + 1) * CH)
-        R.s1[p, 0:CH] = means[rows].astype(BF16)
-        R.s1[p, CH : CH + 16] = split_row(as_row(log_weights[rows], 0), 16)
-
     def scatter_copies(src, dst, send, recv):
         return [
             rcopy(src.at[lax.rem(r + o, G)], dst.at[o - 1], send.at[o - 1], recv.at[o - 1], plane_dev(o))
@@ -253,7 +241,21 @@
         for copy in copies:
             copy.wait_recv()
 
-    scatter_1 = start(scatter_copies(R.s1, R.r1, R.s1_s, R.s1_r))
+    kv_own = R.kvx[1 : NS + 1].reshape(NS * WIN, WIN)
+    R.lg[...] = mm_t(R.wt[...], kv_own).reshape(G, CH, NS * WIN)
+    scatter_1 = scatter_copies(R.s1, R.r1, R.s1_s, R.s1_r)
+    turns = (*far_first(G), 0)
+    for first in range(0, G, G // 2):
+        chunks = [lax.rem(r + o, G) for o in turns[first : first + G // 2]]
+        peaks = [jnp.max(R.lg[p], axis=1, keepdims=True) for p in chunks]
+        expos = [jnp.exp(R.lg[p] - peak) for p, peak in zip(chunks, peaks)]
+        totals = [jnp.sum(expo, axis=1, keepdims=True) for expo in expos]
+        sums = mm(jnp.concatenate([expo.astype(BF16) for expo in expos], axis=0), kv_own)
+        for i, (p, peak, total) in enumerate(zip(chunks, peaks, totals)):
+            R.s1[p, 0:CH] = (sums[i * CH : (i + 1) * CH] / total).astype(BF16)
+            R.s1[p, CH : CH + 16] = split_row(as_row(peak + jnp.log(total), 0), 16)
+        start(scatter_1[first : first + G // 2])
+
 
     halo = start(
         [
@@ -457,24 +459,29 @@
     arrive(gather_2)
     column_row = row_of([join_rows(R.gkv[p, CH : CH + 16]) for p in range(G)])
     grads = R.gkv[:, 0:CH].reshape(LANDMARKS, WIN)
-    for s in every:
-        R.dl[s] = (R.wgt[s] * (mm_t(R.kvx[s + 1], grads) - column_row)).astype(BF16)
-
     turn = lax.rem(y, half) + jnp.where(core_in == c, 0, half // 2)
     segs = [2 * lax.rem(turn + o, half) + i for o in (*far_first(half), 0) for i in range(2)]
 
+    def logit_grads(segs):
+        for s in segs:
+            R.dl[s] = (R.wgt[s] * (mm_t(R.kvx[s + 1], grads) - column_row)).astype(BF16)
+
     def send_kv_grads(segs):
         for s in segs:
             R.km[s] = (mm(R.wgb[s], grads) + mm(R.dl[s], R.wt[...]) + R.dkv[s + 1]).astype(BF16)
         for s in segs:
             send_out(s, R.km, R.ki, R.k_s, R.k_r)
 
+    logit_grads(segs[: NS // 2])
     send_kv_grads(segs[: NS // 2])
+    logit_grads(segs[NS // 2 :])
     arrive(gather_c)
-    R.nt[y] = functools.reduce(lambda a, b: a + b, [R.ct[p] for p in range(G)])
+    R.nm[...] = functools.reduce(lambda a, b: a + b, [R.ct[p] for p in range(G)])
+    own_norm = pltpu.make_async_copy(R.nm, R.nt.at[y], R.own_s.at[1])
+    own_norm.start()
     norm_copies = start(
         [
-            rcopy(R.nt.at[y], R.nt.at[y], R.n_s.at[o - 1], R.n_r.at[o - 1], (x, z, lax.rem(y + o, Y), c))
+            rcopy(R.nm, R.nt.at[y], R.n_s.at[o - 1], R.n_r.at[o - 1], (x, z, lax.rem(y + o, Y), c))
             for o in far_first(Y)
         ]
     )
@@ -489,27 +496,15 @@
             for o in far_first(N)
         ]
     )
-    R.pi[n] = R.pm[n]
+    own_proj = pltpu.make_async_copy(R.pm.at[n], R.pi.at[n], R.own_s.at[0])
+    own_proj.start()
     send_kv_grads(segs[NS // 2 :])
     for h in range(Y):
         rcopy(R.km.at[0], R.ki.at[h], R.k_s.at[0], R.k_r.at[h], (x, z, y, c)).wait_recv()
-    for pair in range(Y // 2):
-        cols = slice(pair * WIN, (pair + 1) * WIN)
-        R.gk_b[:, cols], R.gv_b[:, cols] = unpack_heads(R.ki[2 * pair], R.ki[2 * pair + 1])
-    store("gk", "gv")
     arrive(proj_copies)
-    for h in range(Y):
-        both = R.pi[2 * h] + R.pi[2 * h + 1]
-        R.gp_b[h, 0:HN] = both[:, 0:DH]
-        R.gp_b[h, HN : 2 * HN] = pltpu.roll(both, DH, 1)[:, 0:DH]
     arrive(norm_copies)
-    sums = functools.reduce(lambda a, b: a + b, [R.nt[h] for h in range(Y)])
-    R.gn_b[0:1] = sums[0:1, 0:DH]
-    R.gn_b[1:2] = sums[1:2, 0:DH]
-    R.gn_b[2:3] = sums[0:1, DH:]
-    R.gn_b[3:4] = sums[1:2, DH:]
-
-    store("gp", "gn")
+    own_proj.wait()
+    own_norm.wait()
     for wait in unsent:
         wait()
     for copy in stores.values():
@@ -517,15 +512,41 @@
 
 
 def store_kernel(count, *refs):
-    src, dst, via = (refs[i * count : (i + 1) * count] for i in range(3))
-    read, written = refs[3 * count :]
-    reads = [pltpu.make_async_copy(src[i], via[i], read.at[i]) for i in range(count)]
-    writes = [pltpu.make_async_copy(via[i], dst[i], written.at[i]) for i in range(count)]
+    src = refs[:count]
+    dst = refs[count : count + 6]
+    got = refs[count + 6 : 2 * count + 6]
+    via = refs[2 * count + 6 : 2 * count + 10]
+    read, written = refs[-2:]
+    reads = [pltpu.make_async_copy(src[i], got[i], read.at[i]) for i in range(count)]
+    out = [got[0], got[1], *via]
+    writes = [pltpu.make_async_copy(out[i], dst[i], written.at[i]) for i in range(6)]
     for copy in reads:
         copy.start()
-    for before, after in zip(reads, writes):
-        before.wait()
-        after.start()
+    for i in range(2):
+        reads[i].wait()
+        writes[i].start()
+    ki, pi, nt = got[2:]
+    gk, gv, gp, gn = via
+    reads[2].wait()
+    for pair in range(ki.shape[0] // 2):
+        cols = slice(pair * WIN, (pair + 1) * WIN)
+        gk[:, cols], gv[:, cols] = unpack_heads(ki[2 * pair], ki[2 * pair + 1])
+    writes[2].start()
+    writes[3].start()
+    reads[3].wait()
+    half = pi.shape[1]
+    for h in range(pi.shape[0] // 2):
+        both = pi[2 * h] + pi[2 * h + 1]
+        gp[h, 0:half] = both[:, 0:DH]
+        gp[h, half : 2 * half] = pltpu.roll(both, DH, 1)[:, 0:DH]
+    writes[4].start()
+    reads[4].wait()
+    sums = functools.reduce(lambda a, b: a + b, [nt[h] for h in range(nt.shape[0])])
+    gn[0:1] = sums[0:1, 0:DH]
+    gn[1:2] = sums[1:2, 0:DH]
+    gn[2:3] = sums[0:1, DH:]
+    gn[3:4] = sums[1:2, DH:]
+    writes[5].start()
     for copy in writes:
         copy.wait()
 
@@ -551,6 +572,7 @@
         qg=((NS, *block), BF16),
         wp=((WIN, LANDMARKS), BF16),
         wt=((LANDMARKS, WIN), BF16),
+        lg=((G, CH, NS * WIN), F32),
         s1=((G, CH + 16, WIN), BF16),
         r1=((G - 1, CH + 16, WIN), BF16),
         s2=((CH + 16, WIN), BF16),
@@ -582,10 +604,8 @@
         wgb=((NS, WIN, LANDMARKS), BF16),
         dl=((NS, WIN, LANDMARKS), BF16),
         km=((NS, *block), BF16),
-        ki=((Y, *block), BF16),
         pm=((N, LN // 2, WIN), F32),
-        pi=((N, LN // 2, WIN), F32),
-        nt=((Y, 8, WIN), F32),
+        nm=((8, WIN), F32),
     )
     counts = dict(
         kv=Y, qg=Y, h=2, s1=G - 1, s2=Z - 1, g1=G - 1, gl=G - 1, s3=G - 1, s4=Z - 1, g2=G - 1, gc=G - 1,
@@ -593,33 +613,34 @@
     )
     sems = {f"{name}_{side}": dma((count,)) for name, count in counts.items() for side in "sr"}
     sems["in_s"] = dma((7,))
-    outs = dict(
+    sems["own_s"] = dma((2,))
+    sems["out_s"] = dma((2,))
+    sent = dict(
         att_o=tokens,
         gq_o=tokens,
-        gk_o=tokens,
-        gv_o=tokens,
-        gp_o=((Y, LN, DH), F32),
-        gn_o=((4, DH), F32),
-    )
-    scratch.update({name[:-2] + "_b": o for name, o in outs.items()})
-    sems["out_s"] = dma((len(outs),))
-    names = ("q_i", "k_i", "v_i", "w_i", "gain_i", "bias_i", "g_i", *outs, *scratch, *sems)
+        ki=((Y, *block), BF16),
+        pi=((N, LN // 2, WIN), F32),
+        nt=((Y, 8, WIN), F32),
+    )
+    scratch.update(att_b=tokens, gq_b=tokens)
+    outs = [tokens, tokens, tokens, tokens, ((Y, LN, DH), F32), ((4, DH), F32)]
+    names = ("q_i", "k_i", "v_i", "w_i", "gain_i", "bias_i", "g_i", *sent, *scratch, *sems)
     results = pl.pallas_call(
         functools.partial(kernel, dims, names),
-        out_shape=[jax.ShapeDtypeStruct(*o) for o in outs.values()],
+        out_shape=[jax.ShapeDtypeStruct(*o) for o in sent.values()],
         in_specs=[pl.BlockSpec(memory_space=pl.ANY)] * 7,
-        out_specs=[pl.BlockSpec(memory_space=pl.ANY)] * len(outs),
+        out_specs=[pl.BlockSpec(memory_space=pl.ANY)] * len(sent),
         scratch_shapes=[pltpu.VMEM(*s) for s in scratch.values()] + list(sems.values()),
         compiler_params=pltpu.CompilerParams(
             collective_id=0, has_side_effects=True, vmem_limit_bytes=60 * 1024 * 1024
         ),
     )(q, k, v, w, gain, bias, g)
     att, gq, gk, gv, gp, gn = pl.pallas_call(
-        functools.partial(store_kernel, len(outs)),
-        out_shape=[jax.ShapeDtypeStruct(*o) for o in outs.values()],
-        in_specs=[pl.BlockSpec(memory_space=pl.ANY)] * len(outs),
+        functools.partial(store_kernel, len(sent)),
+        out_shape=[jax.ShapeDtypeStruct(*o) for o in outs],
+        in_specs=[pl.BlockSpec(memory_space=pl.ANY)] * len(sent),
         out_specs=[pl.BlockSpec(memory_space=pl.ANY)] * len(outs),
-        scratch_shapes=[pltpu.VMEM(*o) for o in outs.values()] + [dma((len(outs),))] * 2,
+        scratch_shapes=[pltpu.VMEM(*o) for o in (*sent.values(), *outs[2:])] + [dma((len(sent),)), dma((len(outs),))],
     )(*results)
     return att, gq, gk, gv, gp.transpose(0, 2, 1)[None], gn
 

time: 68.1 us -> 67.6 us (level)
  no operation moved by 1% of the time
where the time goes in v5:
time: 67.6 us; the launch traced here: 67.5 us
  Pallas kernels  66.8 us (99%)
    pallas_call x1, Pallas kernels, layer(): pl.pallas_call(functools.partial(kernel, dims, names), out_shape=[jax.Sha...  64.8 us
    pallas_call x1, Pallas kernels, layer(): pl.pallas_call(functools.partial(store_kernel, len(sent)), out_shape=[jax...  2.05 us

profile of v5, /device:TPU:1, one launch (start us, length us, event | category | flops | bytes accessed | tf_op | source)
XLA Modules:
  0.0 67.5 jit_solution(4174180246157560411)
XLA Ops:
  0.6 64.8 %shard_map.118 = (bf16[128,512]{1,0:T(8,128)(2,1)}, bf16[128,512]{1,0:T(8,128)(2,1)}, bf16[8,128,128]{2,1,0:T(8,128)(2,1)}, f32[16,8,128]{2,1,0:T(8,128)}, f32[8,8,128]{2,1,0:T(8,128)}) custom-call(bf16[128,512]{1,0:T(8,128)(2,1)} %refs_0_.1, bf16[128,512]{1,0:T(8,128)(2,1)} %refs_1_.1, bf16[128,512]{1,0:T(8,128)(2,1)} %refs_2_.1, ...), custom_call_target="tpu_custom_call" | custom-call | tf_op jit(solution)/shard_map/pallas_call | solution.py:628
  65.4 2.1 %shard_map.119 = (bf16[128,512]{1,0:T(8,128)(2,1)}, bf16[128,512]{1,0:T(8,128)(2,1)}, bf16[128,512]{1,0:T(8,128)(2,1)}, bf16[128,512]{1,0:T(8,128)(2,1)}, f32[8,16,64]{2,1,0:T(8,128)}, /*index=5*/f32[4,64]{1,0:T(4,128)}) custom-call(bf16[128,512]{1,0:T(8,128)(2,1)} %get-tuple-element.17.refs_0_, bf16[128,512]{1,0:T(8,128)(2,1)} %get-tuple-element.18.refs_1_, ...), custom_call_target="tpu_custom_call" | custom-call | tf_op jit(solution)/shard_map/pallas_call | solution.py:638

commit v6 on v5

--- a/solution.py
+++ b/solution.py
@@ -143,29 +143,21 @@
             )
             stores[name].start()
 
+    barrier = pltpu.get_barrier_semaphore()
+    partners = [z_dev(o) for o in far_first(Z)]
+    partners += [inner_dev(lax.rem(n + o, N)) for o in far_first(N)]
+    partners += [(lax.rem(x + o, X), z, y, core) for o in far_first(X) for core in range(2)]
+    partners.append(far)
+    for partner in partners:
+        pl.semaphore_signal(barrier, 1, device_id=partner, device_id_type=pl.DeviceIdType.MESH)
+    count = len(partners)
+
     loads = {}
     for i, (name, src) in enumerate(
         (("k", R.k_i), ("v", R.v_i), ("q", R.q_i), ("g", R.g_i), ("w", R.w_i.at[y]), ("gain", R.gain_i), ("bias", R.bias_i))
     ):
         loads[name] = pltpu.make_async_copy(src, getattr(R, name), R.in_s.at[i])
         loads[name].start()
-
-    barrier = pltpu.get_barrier_semaphore()
-    count = 0
-    for o in range(1, N):
-        pl.semaphore_signal(barrier, 1, device_id=inner_dev(lax.rem(n + o, N)), device_id_type=pl.DeviceIdType.MESH)
-        count += 1
-    for xo in range(1, X):
-        for c2 in range(2):
-            pl.semaphore_signal(
-                barrier, 1, device_id=(lax.rem(x + xo, X), z, y, c2), device_id_type=pl.DeviceIdType.MESH
-            )
-            count += 1
-    for o in range(1, Z):
-        pl.semaphore_signal(barrier, 1, device_id=z_dev(o), device_id_type=pl.DeviceIdType.MESH)
-        count += 1
-    pl.semaphore_signal(barrier, 1, device_id=far, device_id_type=pl.DeviceIdType.MESH)
-    count += 1
 
     loads["k"].wait()
     loads["v"].wait()

time: 67.6 us -> 67.2 us (level)
  no operation moved by 1% of the time
where the time goes in v6:
time: 67.2 us; the launch traced here: 67.1 us
  Pallas kernels  66.4 us (99%)
    pallas_call x1, Pallas kernels, layer(): pl.pallas_call(functools.partial(kernel, dims, names), out_shape=[jax.Sha...  64.4 us
    pallas_call x1, Pallas kernels, layer(): pl.pallas_call(functools.partial(store_kernel, len(sent)), out_shape=[jax...  2.05 us

profile of v6, /device:TPU:1, one launch (start us, length us, event | category | flops | bytes accessed | tf_op | source)
XLA Modules:
  0.0 67.1 jit_solution(15194056803069167052)
XLA Ops:
  0.6 64.4 %shard_map.118 = (bf16[128,512]{1,0:T(8,128)(2,1)}, bf16[128,512]{1,0:T(8,128)(2,1)}, bf16[8,128,128]{2,1,0:T(8,128)(2,1)}, f32[16,8,128]{2,1,0:T(8,128)}, f32[8,8,128]{2,1,0:T(8,128)}) custom-call(bf16[128,512]{1,0:T(8,128)(2,1)} %refs_0_.1, bf16[128,512]{1,0:T(8,128)(2,1)} %refs_1_.1, bf16[128,512]{1,0:T(8,128)(2,1)} %refs_2_.1, ...), custom_call_target="tpu_custom_call" | custom-call | tf_op jit(solution)/shard_map/pallas_call | solution.py:620
  65.0 2.1 %shard_map.119 = (bf16[128,512]{1,0:T(8,128)(2,1)}, bf16[128,512]{1,0:T(8,128)(2,1)}, bf16[128,512]{1,0:T(8,128)(2,1)}, bf16[128,512]{1,0:T(8,128)(2,1)}, f32[8,16,64]{2,1,0:T(8,128)}, /*index=5*/f32[4,64]{1,0:T(4,128)}) custom-call(bf16[128,512]{1,0:T(8,128)(2,1)} %get-tuple-element.17.refs_0_, bf16[128,512]{1,0:T(8,128)(2,1)} %get-tuple-element.18.refs_1_, ...), custom_call_target="tpu_custom_call" | custom-call | tf_op jit(solution)/shard_map/pallas_call | solution.py:630
